TPU v7x, 32 devices: a whole 2x2x4 slice. The times are simulated.
32 devices in a mesh: parts: 2 (over y), patch: 4 (over z), sub: 4 (over x, core).
Axes of the slice: x: 2, y: 2, z: 4, core: 2. Of those that a mesh axis runs over, the one named last changes fastest.
Arguments:
- node_latents: bfloat16 [4096, 512], P(('parts', 'patch', 'sub')), parts along dimension 0, may hold values from -6 to 6
- edge_latents: bfloat16 [16384, 512], P(('parts', 'patch', 'sub')), parts along dimension 0, may hold values from -6 to 6
- coarse_edges: bfloat16 [2048, 512], P(('parts', 'patch', 'sub')), parts along dimension 0, may hold values from -6 to 6
- w_edge_in: bfloat16 [1536, 512], replicated, may hold values from -0.15625 to 0.15625
- w_edge_out: bfloat16 [512, 512], replicated, may hold values from -0.25 to 0.25
- w_node_in: bfloat16 [1024, 512], replicated, may hold values from -0.1875 to 0.1875
- w_node_out: bfloat16 [512, 512], replicated, may hold values from -0.25 to 0.25
- fine_senders: int32 [16384], P(('parts', 'patch', 'sub')), parts along dimension 0, may hold values from 0 to 159
- fine_receivers: int32 [16384], P(('parts', 'patch', 'sub')), parts along dimension 0, may hold values from -1 to 127, as said below
- halo_lists: int32 [32, 2, 16], P(('parts', 'patch', 'sub')), parts along dimension 0, may hold values from 0 to 127, as said below
- coarse_senders: int32 [2048], P(('parts', 'patch', 'sub')), parts along dimension 0, may hold values from 0 to 63
- coarse_receivers: int32 [2048], P(('parts', 'patch', 'sub')), parts along dimension 0, may hold values from 0 to 63
Outputs:
- new_nodes: bfloat16 [4096, 512], P(('parts', 'patch', 'sub')), parts along dimension 0
- new_edges: bfloat16 [16384, 512], P(('parts', 'patch', 'sub')), parts along dimension 0
- new_coarse: bfloat16 [2048, 512], P(('parts', 'patch', 'sub')), parts along dimension 0
There are 2 independent parts, one for each index of `parts`. A program takes and returns all parts, laid end to end along the dimension named above; an argument that names none is the same for every part. Nothing has to cross between parts.
Inputs may be any that keep to these rules, and one draw needn't show every extreme that they name: `fine_receivers`: in each device's block of 512 slots the used slots come first and name a local row; the rest hold -1. At least half of a device's slots are used, and some device uses all of them. `halo_lists`: each of a device's two lists holds 16 distinct local rows.
All inputs are finite; a program needn't handle non-finite values.
Results may differ from a plain program's by a relative error of at most 0.0053.
Values may be sent and summed in bfloat16 or wider, within the bound.
No kernel may reach another device: no remote copies, remote signals or barrier semaphores. Data moves between devices by JAX's collectives and lax.ppermute only.
A program may use at most 64 MiB of HBM per device.

v0:
```python
import jax
import jax.numpy as jnp
from jax import lax
from jax.experimental import pallas as pl
from jax.experimental.pallas import tpu as pltpu
from jax.sharding import PartitionSpec as P

CO_DEV = 4
GROUP_AXES = ("patch", "sub")
TOP = 16
STEP = 256
MIB = 1 << 20
ANY = pl.BlockSpec(memory_space=pl.ANY)
VMEM = pl.BlockSpec(memory_space=pltpu.VMEM)
BF16, F32 = jnp.bfloat16, jnp.float32


def first_order(group):
    return list(reversed(range(group)))


def second_order(group):
    return [(i + group // 2) % group for i in range(group)]


def pair(value, first):
    devices = lax.axis_size(GROUP_AXES)
    pairs = [(i, (i + 1) % devices) for i in range(first, devices, 2)]
    return lax.ppermute(value, GROUP_AXES, pairs + [(b, a) for a, b in pairs])


def dot(a, b):
    return jnp.dot(a, b, preferred_element_type=F32)


def dot_t(a, b):
    return lax.dot_general(a, b, (((0,), (0,)), ((), ())), preferred_element_type=F32)


def onehot_t(rows, ids):
    at = lax.broadcasted_iota(jnp.int32, (rows, ids.shape[1]), 0)
    return jnp.where(at == ids, 1.0, 0.0).astype(BF16)


def silu(v):
    half = 0.5 * v
    return half + half * jnp.tanh(half)


def norm_parts(values):
    mean = jnp.mean(values, axis=-1, keepdims=True)
    centred = values - mean
    return centred, lax.rsqrt(jnp.mean(centred * centred, axis=-1, keepdims=True) + 1e-05)


def head_kernel(nodes_hbm, heads_ref, rows_ref, sem):
    copy = pltpu.make_async_copy(nodes_hbm.at[pl.ds(0, TOP)], rows_ref, sem)
    copy.start()
    copy.wait()
    head = rows_ref[0:CO_DEV, :]
    for at in range(heads_ref.shape[0]):
        heads_ref[at] = head


def start_copies(sources, targets, sems):
    copies = [pltpu.make_async_copy(a, b, sems.at[i]) for i, (a, b) in enumerate(zip(sources, targets))]
    for copy in copies:
        copy.start()
    return copies


def load_kernel(
    nodes_hbm, lists_hbm, cedges_hbm, w_in_hbm, csend_hbm, crecv_hbm, w_out_hbm, after,
    nodes_ref, cedges_ref, w_ends_ref, w_out_ref, even_ref, odd_ref, gather_ref, picks_ref, part_ref,
    lists_ref, w_self_ref, csend_ref, crecv_ref, sems,
):
    width = nodes_ref.shape[1]
    copies = start_copies(
        [
            nodes_hbm, lists_hbm, cedges_hbm, w_in_hbm.at[pl.ds(0, width)], csend_hbm, crecv_hbm,
            w_in_hbm.at[pl.ds(width, 2 * width)], w_out_hbm,
        ],
        [nodes_ref, lists_ref, cedges_ref, w_self_ref, csend_ref, crecv_ref, w_ends_ref, w_out_ref],
        sems,
    )
    for copy in copies[:2]:
        copy.wait()
    nodes = nodes_ref[...]
    count = nodes.shape[0]
    lists = lists_ref[0]
    me = lax.axis_index(GROUP_AXES)
    odd = me % 2
    first = lists[0:1, :] * (1 - odd) + lists[1:2, :] * odd
    second = lists[1:2, :] * (1 - odd) + lists[0:1, :] * odd
    even_ref[...] = dot_t(onehot_t(count, first), nodes).astype(BF16)
    odd_ref[...] = dot_t(onehot_t(count, second), nodes).astype(BF16)
    for copy in copies[2:6]:
        copy.wait()
    part_ref[...] = dot(cedges_ref[...], w_self_ref[...])
    rows, ids = picks_ref.shape
    at = lax.broadcasted_iota(jnp.int32, (rows, ids), 0)
    node = (rows // CO_DEV - 1 - at // CO_DEV) * CO_DEV + at % CO_DEV
    send = jnp.where(node == csend_ref[...], 1.0, 0.0).astype(BF16)
    recv = jnp.where(node == crecv_ref[...], 1.0, 0.0).astype(BF16)
    picks_ref[...] = onehot_t(rows, crecv_ref[...])
    across = lax.broadcasted_iota(jnp.int32, (rows, rows), 0) == lax.broadcasted_iota(jnp.int32, (rows, rows), 1)
    eye = jnp.where(across, 1.0, 0.0).astype(BF16)
    gather_ref[0:ids, :] = dot_t(send, eye).astype(BF16)
    gather_ref[ids:, :] = dot_t(recv, eye).astype(BF16)
    for copy in copies[6:]:
        copy.wait()


def coarse_kernel(
    lat_ref, edges_ref, part_ref, gather_ref, picks_ref, w_ends_ref, w_out_ref, new_ref, sums_hbm, sums_ref, sem
):
    count, width = edges_ref.shape
    blocks = lat_ref.shape[0]
    lat = jnp.concatenate([lat_ref[at].astype(F32) for at in range(blocks)], axis=0).astype(BF16)
    ends = dot(gather_ref[...], lat).astype(BF16)
    ends = jnp.concatenate([ends[0:count], ends[count:]], axis=1)
    hidden = silu(part_ref[...] + dot(ends, w_ends_ref[...])).astype(BF16)
    centred, scale = norm_parts(dot(hidden, w_out_ref[...]))
    new = (edges_ref[...].astype(F32) + centred * scale).astype(BF16)
    new_ref[...] = new
    sums = dot(picks_ref[...], new).astype(BF16)
    for at, owner in enumerate(second_order(blocks)):
        sums_ref[at] = sums[owner * CO_DEV : (owner + 1) * CO_DEV, :]
    copy = pltpu.make_async_copy(sums_ref, sums_hbm, sem)
    copy.start()
    copy.wait()


def fine_kernel(
    even_ref, nodes_ref, odd_ref, w_ends_ref, w_out_ref, coarse_ref,
    edges_hbm, w_in_hbm, send_hbm, recv_hbm, wn_in_hbm, wn_out_hbm, after,
    new_hbm, coarse_hbm, out_ref, agg_ref, npart_ref, wn_agg_ref, wn_out_ref,
    edges_ref, w_self_ref, send_ref, recv_ref, wn_self_ref, new_ref, sems, out_sems,
):
    nodes = nodes_ref[...]
    count, width = nodes.shape
    copies = start_copies(
        [
            send_hbm, recv_hbm, edges_hbm, w_in_hbm.at[pl.ds(0, width)],
            wn_in_hbm.at[pl.ds(0, width)], wn_in_hbm.at[pl.ds(width, width)], wn_out_hbm,
        ],
        [send_ref, recv_ref, edges_ref, w_self_ref, wn_self_ref, wn_agg_ref, wn_out_ref],
        sems,
    )
    odd = (lax.axis_index(GROUP_AXES) % 2).astype(F32)
    met, other = even_ref[...].astype(F32), odd_ref[...].astype(F32)
    prev = (met * odd + other * (1.0 - odd)).astype(BF16)
    following = (other * odd + met * (1.0 - odd)).astype(BF16)
    extended = jnp.concatenate([prev, nodes, following], axis=0)
    ones = jnp.ones((count, 128), BF16)
    total = jnp.zeros((count, width), F32)
    for copy in copies[:2]:
        copy.wait()
    outs = [pltpu.make_async_copy(coarse_ref, coarse_hbm, out_sems.at[0])]
    outs[0].start()
    for at in range(0, edges_ref.shape[0], STEP):
        rows = pl.ds(at, STEP)
        picks = onehot_t(count, recv_ref[:, rows])
        senders = dot_t(onehot_t(extended.shape[0], send_ref[:, rows]), extended).astype(BF16)
        receivers = dot_t(picks, nodes).astype(BF16)
        valid = dot_t(picks, ones)[:, 0:1]
        pre = dot(jnp.concatenate([senders, receivers], axis=1), w_ends_ref[...])
        if at == 0:
            for copy in copies[2:4]:
                copy.wait()
        edges = edges_ref[rows, :]
        pre = pre + dot(edges, w_self_ref[...])
        hidden = silu(pre).astype(BF16)
        centred, scale = norm_parts(dot(hidden, w_out_ref[...]))
        new = (edges.astype(F32) + centred * (scale * valid)).astype(BF16)
        new_ref[rows, :] = new
        copy = pltpu.make_async_copy(new_ref.at[rows], new_hbm.at[rows], out_sems.at[at // STEP + 1])
        copy.start()
        outs.append(copy)
        total = total + dot(picks, new)
    agg_ref[...] = total[0:TOP]
    for copy in copies[4:]:
        copy.wait()
    pre = dot(nodes, wn_self_ref[...])
    npart_ref[...] = pre[0:TOP]
    pre = pre + dot(total.astype(BF16), wn_agg_ref[...])
    hidden = silu(pre).astype(BF16)
    centred, scale = norm_parts(dot(hidden, wn_out_ref[...]))
    out_ref[...] = (nodes.astype(F32) + centred * scale).astype(BF16)
    for copy in outs:
        copy.wait()


def top_kernel(got_ref, agg_ref, part_ref, nodes_ref, wn_agg_ref, wn_out_ref, rest_ref, out_ref):
    width = agg_ref.shape[1]
    terms = [got_ref[at].astype(F32) for at in range(got_ref.shape[0])]
    while len(terms) > 1:
        half = len(terms) // 2
        terms = [a + b for a, b in zip(terms[:half], terms[half:])] + terms[2 * half :]
    sums = jnp.concatenate([terms[0], jnp.zeros((TOP - CO_DEV, width), F32)], axis=0)
    agg = (agg_ref[...] + sums).astype(BF16)
    hidden = silu(part_ref[...] + dot(agg, wn_agg_ref[...])).astype(BF16)
    centred, scale = norm_parts(dot(hidden, wn_out_ref[...]))
    out_ref[...] = (nodes_ref[0:TOP, :].astype(F32) + centred * scale).astype(BF16)


def in_hbm(*arrays):
    return [pltpu.with_memory_space_constraint(a, pltpu.HBM) for a in arrays]


def cost(flops, moved=0):
    return pl.CostEstimate(flops=flops, bytes_accessed=moved, transcendentals=0)


def call(kernel, name, outs, ins, out_specs=None, scratch=(), hbm=(), flops=0, **more):
    return pl.pallas_call(
        kernel,
        out_shape=outs,
        in_specs=[ANY if i in hbm else VMEM for i in range(len(ins))],
        out_specs=[VMEM] * len(outs) if out_specs is None else out_specs,
        scratch_shapes=scratch,
        compiler_params=pltpu.CompilerParams(vmem_limit_bytes=16 * MIB),
        cost_estimate=cost(flops),
        name=name,
        **more,
    )(*ins)


def body(
    node_latents,
    edge_latents,
    coarse_edges,
    w_edge_in,
    w_edge_out,
    w_node_in,
    w_node_out,
    fine_senders,
    fine_receivers,
    halo_lists,
    coarse_senders,
    coarse_receivers,
):
    count, width = node_latents.shape
    edge_count = edge_latents.shape[0]
    cedge_count = coarse_edges.shape[0]
    halo = halo_lists.shape[2]
    group = lax.axis_size(GROUP_AXES)
    coarse_count = group * CO_DEV
    shape = jax.ShapeDtypeStruct
    like = lambda a: shape(a.shape, a.dtype)
    vmem = pltpu.VMEM
    dma = pltpu.SemaphoreType.DMA
    square = 2 * width * width
    blocks = shape((group, CO_DEV, width), BF16)
    ids = lambda a: a[None, :]

    (heads,) = call(
        head_kernel, "head", (blocks,), in_hbm(node_latents), hbm=(0,), scratch=[vmem((TOP, width), BF16), dma(())],
    )
    lat = lax.all_to_all(heads, GROUP_AXES, 0, 0, axis_index_groups=[first_order(group)])
    nodes, cedges, w_ends, w_out, to_even, to_odd, gather, picks, coarse_part = call(
        load_kernel,
        "load",
        (
            like(node_latents),
            like(coarse_edges),
            shape((2 * width, width), BF16),
            like(w_edge_out),
            shape((halo, width), BF16),
            shape((halo, width), BF16),
            shape((2 * cedge_count, coarse_count), BF16),
            shape((coarse_count, cedge_count), BF16),
            shape((cedge_count, width), F32),
        ),
        in_hbm(node_latents, halo_lists, coarse_edges, w_edge_in, ids(coarse_senders), ids(coarse_receivers), w_edge_out)
        + [heads],
        hbm=range(8),
        scratch=[
            vmem(halo_lists.shape, jnp.int32), vmem((width, width), BF16),
            vmem((1, cedge_count), jnp.int32), vmem((1, cedge_count), jnp.int32), dma((8,)),
        ],
        flops=edge_count * square,
    )
    from_even, from_odd = pair(to_even, 0), pair(to_odd, 1)
    new_coarse, sums = call(
        coarse_kernel, "coarse", (like(coarse_edges), blocks),
        [lat, cedges, coarse_part, gather, picks, w_ends, w_out], out_specs=[VMEM, ANY],
        scratch=[vmem(blocks.shape, BF16), dma(())],
    )
    got = lax.all_to_all(sums, GROUP_AXES, 0, 0, axis_index_groups=[second_order(group)])
    new_edges, new_coarse, rest, agg, node_part, wn_agg, wn_out = call(
        fine_kernel,
        "fine",
        (
            like(edge_latents),
            like(coarse_edges),
            like(node_latents),
            shape((TOP, width), F32),
            shape((TOP, width), F32),
            shape((width, width), BF16),
            like(w_node_out),
        ),
        [from_even, nodes, from_odd, w_ends, w_out, new_coarse]
        + in_hbm(edge_latents, w_edge_in, ids(fine_senders), ids(fine_receivers), w_node_in, w_node_out)
        + [sums],
        hbm=range(6, 13),
        out_specs=[ANY] * 2 + [VMEM] * 5,
        scratch=[
            vmem(edge_latents.shape, BF16), vmem((width, width), BF16), vmem((1, edge_count), jnp.int32),
            vmem((1, edge_count), jnp.int32), vmem((width, width), BF16), vmem(edge_latents.shape, BF16), dma((7,)),
            dma((edge_count // STEP + 1,)),
        ],
        flops=64 * edge_count * square,
    )
    new_nodes = pl.pallas_call(
        top_kernel,
        grid=(1,),
        out_shape=like(node_latents),
        in_specs=[VMEM] * 6 + [ANY],
        out_specs=pl.BlockSpec((TOP, width), lambda i: (0, 0)),
        input_output_aliases={6: 0},
        compiler_params=pltpu.CompilerParams(vmem_limit_bytes=16 * MIB),
        name="top",
    )(got, agg, node_part, nodes, wn_agg, wn_out, rest)
    return (new_nodes, new_edges, new_coarse)


def solution(mesh):
    rows = P(("parts", "patch", "sub"), None)
    ids = P(("parts", "patch", "sub"))
    in_specs = (
        rows, rows, rows, P(), P(), P(), P(), ids, ids, P(("parts", "patch", "sub"), None, None), ids, ids,
    )
    return jax.shard_map(body, mesh=mesh, in_specs=in_specs, out_specs=(rows, rows, rows), check_vma=False)
```

profile of v0, /device:TPU:0, one launch (start us, length us, event | category | flops | bytes accessed | tf_op | source)
XLA Modules:
  0.0 27.2 jit_solution(2305340553707028695)
XLA Ops:
  0.6 1.4 %head.1.after = bf16[16,4,512]{2,1,0:T(4,128)(2,1)} custom-call(bf16[128,512]{1,0:T(8,128)(2,1)} %nodes_hbm.3), custom_call_target="tpu_custom_call" | custom-call | tf_op jit(solution)/shard_map/head/pallas_call | solution.py:216
  2.0 8.8 %all-to-all-start = ((bf16[16,4,512]{2,1,0:T(4,128)(2,1)}), bf16[16,4,512]{2,1,0:T(4,128)(2,1)S(1)}, u32[]{:S(2)}, u32[]{:S(2)}) async-start(bf16[16,4,512]{2,1,0:T(4,128)(2,1)} %head.1.after), calls=%async_computation | async-start | bytes 131072 | tf_op jit(solution)/shard_map/all_to_all | solution.py:260
  10.8 1.7 %load.1 = (bf16[128,512]{1,0:T(8,128)(2,1)S(1)}, bf16[64,512]{1,0:T(8,128)(2,1)S(1)}, bf16[1024,512]{1,0:T(8,128)(2,1)S(1)}, bf16[512,512]{1,0:T(8,128)(2,1)S(1)...) custom-call(bf16[128,512]{1,0:T(8,128)(2,1)} %nodes_hbm.3, ...), custom_call_target="tpu_custom_call" | custom-call | flops 268435456 | tf_op jit(solution)/shard_map/load/pallas_call | solution.py:216
  12.6 0.1 collective-permute-start
  12.7 0.6 %collective-permute-start.1 = (bf16[16,512]{1,0:T(8,128)(2,1)S(1)}, bf16[16,512]{1,0:T(8,128)(2,1)S(1)}, u32[]{:S(2)}, u32[]{:S(2)}) collective-permute-start(bf16[16,512]{1,0:T(8,128)(2,1)S(1)} %get-tuple-element.30), channel_id=1, source_target_pairs={{1,2},{3,4},{5,6},{7,8},{9,10},{11,12},{13,14},{15,0},{2,1},{4,3},... | collective-permute-start | bytes 49160 | tf_op jit(solution)/shard_map/ppermute | solution.py:29
  13.3 0.3 %all-to-all-done.lat_ref = bf16[16,4,512]{2,1,0:T(4,128)(2,1)S(1)} async-done(((bf16[16,4,512]{2,1,0:T(4,128)(2,1)}), bf16[16,4,512]{2,1,0:T(4,128)(2,1)S(1)}, u32[]{:S(2)}, u32[]{:S(2)}) %all-to-all-start) | async-done | bytes 65568 | tf_op jit(solution)/shard_map/all_to_all | solution.py:260
  13.7 1.5 %coarse.1 = (bf16[64,512]{1,0:T(8,128)(2,1)S(1)}, bf16[16,4,512]{2,1,0:T(4,128)(2,1)}) custom-call(bf16[16,4,512]{2,1,0:T(4,128)(2,1)S(1)} %all-to-all-done.lat_ref, bf16[64,512]{1,0:T(8,128)(2,1)S(1)} %get-tuple-element.21.edges_ref, f32[64,512]{1,0:T(8,128)S(1)} %get-tuple-element.22.part_ref, bf16[128,64]{1,0:T(8,128)(2,1)S(1)} %get-tuple-element.23.gather_ref, ...), custom_call_target="tpu_custom_call" | custom-call | tf_op jit(solution)/shard_map/coarse/pallas_call | solution.py:216
  15.2 6.0 %all-to-all-start.1 = ((bf16[16,4,512]{2,1,0:T(4,128)(2,1)}), bf16[16,4,512]{2,1,0:T(4,128)(2,1)S(1)}, u32[]{:S(2)}, u32[]{:S(2)}) async-start(bf16[16,4,512]{2,1,0:T(4,128)(2,1)} %get-tuple-element.27.after), calls=%async_computation.1 | async-start | bytes 131072 | tf_op jit(solution)/shard_map/all_to_all | solution.py:290
  21.2 0.0 collective-permute-done.even_ref
  21.2 0.0 collective-permute-done.1.odd_ref
  21.2 4.8 %fine.1 = (bf16[512,512]{1,0:T(8,128)(2,1)}, bf16[64,512]{1,0:T(8,128)(2,1)}, bf16[128,512]{1,0:T(8,128)(2,1)}, f32[16,512]{1,0:T(8,128)S(1)}, f32[16,512]{1,0:T...) custom-call(bf16[16,512]{1,0:T(8,128)(2,1)S(1)} %collective-permute-done.even_ref, ...), custom_call_target="tpu_custom_call" | custom-call | flops 17179869184 | tf_op jit(solution)/shard_map/fine/pallas_call | solution.py:216
  26.0 0.0 all-to-all-done.1.got_ref
  26.0 1.1 %top.1 = bf16[128,512]{1,0:T(8,128)(2,1)} custom-call(bf16[16,4,512]{2,1,0:T(4,128)(2,1)S(1)} %all-to-all-done.1.got_ref, f32[16,512]{1,0:T(8,128)S(1)} %get-tuple-element.32.agg_ref, f32[16,512]{1,0:T(8,128)S(1)} %get-tuple-element.33.part_ref, bf16[128,512]{1,0:T(8,128)(2,1)S(1)} %get-tuple-element.29.nodes_ref, ...), custom_call_target="tpu_custom_call", output_to_operand_aliasing={{}: (6, {})} | custom-call | tf_op jit(solution)/shard_map/top/pallas_call | solution.py:315
Async XLA Ops:
  2.0 11.7 %all-to-all-start = ((bf16[16,4,512]{2,1,0:T(4,128)(2,1)}), bf16[16,4,512]{2,1,0:T(4,128)(2,1)S(1)}, u32[]{:S(2)}, u32[]{:S(2)}) async-start(bf16[16,4,512]{2,1,0:T(4,128)(2,1)} %head.1.after), calls=%async_computation | async-start | bytes 131072 | tf_op jit(solution)/shard_map/all_to_all | solution.py:260
  12.6 8.6 %collective-permute-start = (bf16[16,512]{1,0:T(8,128)(2,1)S(1)}, bf16[16,512]{1,0:T(8,128)(2,1)S(1)}, u32[]{:S(2)}, u32[]{:S(2)}) collective-permute-start(bf16[16,512]{1,0:T(8,128)(2,1)S(1)} %get-tuple-element.28), channel_id=1, source_target_pairs={{0,1},{2,3},{4,5},{6,7},{8,9},{10,11},{12,13},{14,15},{1,0},{3,2},... | collective-permute-start | bytes 49160 | tf_op jit(solution)/shard_map/ppermute | solution.py:29
  12.7 8.5 %collective-permute-start.1 = (bf16[16,512]{1,0:T(8,128)(2,1)S(1)}, bf16[16,512]{1,0:T(8,128)(2,1)S(1)}, u32[]{:S(2)}, u32[]{:S(2)}) collective-permute-start(bf16[16,512]{1,0:T(8,128)(2,1)S(1)} %get-tuple-element.30), channel_id=1, source_target_pairs={{1,2},{3,4},{5,6},{7,8},{9,10},{11,12},{13,14},{15,0},{2,1},{4,3},... | collective-permute-start | bytes 49160 | tf_op jit(solution)/shard_map/ppermute | solution.py:29
  15.2 10.8 %all-to-all-start.1 = ((bf16[16,4,512]{2,1,0:T(4,128)(2,1)}), bf16[16,4,512]{2,1,0:T(4,128)(2,1)S(1)}, u32[]{:S(2)}, u32[]{:S(2)}) async-start(bf16[16,4,512]{2,1,0:T(4,128)(2,1)} %get-tuple-element.27.after), calls=%async_computation.1 | async-start | bytes 131072 | tf_op jit(solution)/shard_map/all_to_all | solution.py:290
where the time goes:
time: 27.6 us; the launch traced here: 27.2 us
  starting transfers between devices  15.6 us (57%)
  Pallas kernels  10.5 us (38%)
  between operations  0.68 us (2%)
  waiting for transfers between devices  0.34 us (1%)
    pallas_call x4, Pallas kernels, call(): pl.pallas_call(kernel, out_shape=outs, in_specs=[ANY if i in hbm else VME...  9.4 us
    all_to_all x1, starting transfers between devices, body(): lax.all_to_all(heads, GROUP_AXES, 0, 0, axis_index_groups=[first_order(gr...  8.84 us
    all_to_all x1, starting transfers between devices, body(): lax.all_to_all(sums, GROUP_AXES, 0, 0, axis_index_groups=[second_order(gr...  6.03 us
    pallas_call x1, Pallas kernels, body(): pl.pallas_call(top_kernel, grid=(1,), out_shape=like(node_latents), in_sp...  1.13 us
    ppermute x2, starting transfers between devices, pair(): return lax.ppermute(value, GROUP_AXES, pairs + [(b, a) for a, b in pairs])  0.75 us
  transfers between devices with their start and end apart: 4, of which 1 were waited for; matrix products, arithmetic and copies ran while one was open for 0% of the time, Pallas kernels for 30%

commit v1 on v0

--- a/solution.py
+++ b/solution.py
@@ -15,12 +15,8 @@
 BF16, F32 = jnp.bfloat16, jnp.float32
 
 
-def first_order(group):
+def order(group):
     return list(reversed(range(group)))
-
-
-def second_order(group):
-    return [(i + group // 2) % group for i in range(group)]
 
 
 def pair(value, first):
@@ -70,17 +66,21 @@
 
 
 def load_kernel(
-    nodes_hbm, lists_hbm, cedges_hbm, w_in_hbm, csend_hbm, crecv_hbm, w_out_hbm, after,
-    nodes_ref, cedges_ref, w_ends_ref, w_out_ref, even_ref, odd_ref, gather_ref, picks_ref, part_ref,
-    lists_ref, w_self_ref, csend_ref, crecv_ref, sems,
+    nodes_hbm, lists_hbm, cedges_hbm, w_in_hbm, csend_hbm, crecv_hbm, w_out_hbm, edges_hbm, send_hbm, recv_hbm, after,
+    nodes_ref, cedges_ref, w_self_ref, w_ends_ref, w_out_ref, edges_ref, send_ref, recv_ref,
+    even_ref, odd_ref, gather_ref, picks_ref, part_ref,
+    lists_ref, csend_ref, crecv_ref, sems,
 ):
     width = nodes_ref.shape[1]
     copies = start_copies(
         [
             nodes_hbm, lists_hbm, cedges_hbm, w_in_hbm.at[pl.ds(0, width)], csend_hbm, crecv_hbm,
-            w_in_hbm.at[pl.ds(width, 2 * width)], w_out_hbm,
+            w_in_hbm.at[pl.ds(width, 2 * width)], w_out_hbm, edges_hbm, send_hbm, recv_hbm,
         ],
-        [nodes_ref, lists_ref, cedges_ref, w_self_ref, csend_ref, crecv_ref, w_ends_ref, w_out_ref],
+        [
+            nodes_ref, lists_ref, cedges_ref, w_self_ref, csend_ref, crecv_ref, w_ends_ref, w_out_ref, edges_ref,
+            send_ref, recv_ref,
+        ],
         sems,
     )
     for copy in copies[:2]:
@@ -124,7 +124,7 @@
     new = (edges_ref[...].astype(F32) + centred * scale).astype(BF16)
     new_ref[...] = new
     sums = dot(picks_ref[...], new).astype(BF16)
-    for at, owner in enumerate(second_order(blocks)):
+    for at, owner in enumerate(order(blocks)):
         sums_ref[at] = sums[owner * CO_DEV : (owner + 1) * CO_DEV, :]
     copy = pltpu.make_async_copy(sums_ref, sums_hbm, sem)
     copy.start()
@@ -132,21 +132,20 @@
 
 
 def fine_kernel(
-    even_ref, nodes_ref, odd_ref, w_ends_ref, w_out_ref, coarse_ref,
-    edges_hbm, w_in_hbm, send_hbm, recv_hbm, wn_in_hbm, wn_out_hbm, after,
+    even_ref, nodes_ref, odd_ref, w_self_ref, w_ends_ref, w_out_ref, edges_ref, send_ref, recv_ref, coarse_ref,
+    wn_in_hbm, wn_out_hbm, after,
     new_hbm, coarse_hbm, out_ref, agg_ref, npart_ref, wn_agg_ref, wn_out_ref,
-    edges_ref, w_self_ref, send_ref, recv_ref, wn_self_ref, new_ref, sems, out_sems,
+    wn_self_ref, new_ref, sems, out_sems,
 ):
     nodes = nodes_ref[...]
     count, width = nodes.shape
     copies = start_copies(
-        [
-            send_hbm, recv_hbm, edges_hbm, w_in_hbm.at[pl.ds(0, width)],
-            wn_in_hbm.at[pl.ds(0, width)], wn_in_hbm.at[pl.ds(width, width)], wn_out_hbm,
-        ],
-        [send_ref, recv_ref, edges_ref, w_self_ref, wn_self_ref, wn_agg_ref, wn_out_ref],
+        [wn_in_hbm.at[pl.ds(0, width)], wn_in_hbm.at[pl.ds(width, width)], wn_out_hbm],
+        [wn_self_ref, wn_agg_ref, wn_out_ref],
         sems,
     )
+    outs = [pltpu.make_async_copy(coarse_ref, coarse_hbm, out_sems.at[0])]
+    outs[0].start()
     odd = (lax.axis_index(GROUP_AXES) % 2).astype(F32)
     met, other = even_ref[...].astype(F32), odd_ref[...].astype(F32)
     prev = (met * odd + other * (1.0 - odd)).astype(BF16)
@@ -154,22 +153,14 @@
     extended = jnp.concatenate([prev, nodes, following], axis=0)
     ones = jnp.ones((count, 128), BF16)
     total = jnp.zeros((count, width), F32)
-    for copy in copies[:2]:
-        copy.wait()
-    outs = [pltpu.make_async_copy(coarse_ref, coarse_hbm, out_sems.at[0])]
-    outs[0].start()
     for at in range(0, edges_ref.shape[0], STEP):
         rows = pl.ds(at, STEP)
         picks = onehot_t(count, recv_ref[:, rows])
         senders = dot_t(onehot_t(extended.shape[0], send_ref[:, rows]), extended).astype(BF16)
         receivers = dot_t(picks, nodes).astype(BF16)
         valid = dot_t(picks, ones)[:, 0:1]
-        pre = dot(jnp.concatenate([senders, receivers], axis=1), w_ends_ref[...])
-        if at == 0:
-            for copy in copies[2:4]:
-                copy.wait()
         edges = edges_ref[rows, :]
-        pre = pre + dot(edges, w_self_ref[...])
+        pre = dot(edges, w_self_ref[...]) + dot(jnp.concatenate([senders, receivers], axis=1), w_ends_ref[...])
         hidden = silu(pre).astype(BF16)
         centred, scale = norm_parts(dot(hidden, w_out_ref[...]))
         new = (edges.astype(F32) + centred * (scale * valid)).astype(BF16)
@@ -179,7 +170,7 @@
         outs.append(copy)
         total = total + dot(picks, new)
     agg_ref[...] = total[0:TOP]
-    for copy in copies[4:]:
+    for copy in copies:
         copy.wait()
     pre = dot(nodes, wn_self_ref[...])
     npart_ref[...] = pre[0:TOP]
@@ -191,8 +182,11 @@
         copy.wait()
 
 
-def top_kernel(got_ref, agg_ref, part_ref, nodes_ref, wn_agg_ref, wn_out_ref, rest_ref, out_ref):
-    width = agg_ref.shape[1]
+def top_kernel(got_ref, agg_ref, part_ref, nodes_ref, wn_agg_ref, wn_out_ref, rest_ref, out_hbm, top_ref, sems):
+    count, width = rest_ref.shape
+    below = pl.ds(TOP, count - TOP)
+    rest = pltpu.make_async_copy(rest_ref.at[below], out_hbm.at[below], sems.at[0])
+    rest.start()
     terms = [got_ref[at].astype(F32) for at in range(got_ref.shape[0])]
     while len(terms) > 1:
         half = len(terms) // 2
@@ -201,7 +195,11 @@
     agg = (agg_ref[...] + sums).astype(BF16)
     hidden = silu(part_ref[...] + dot(agg, wn_agg_ref[...])).astype(BF16)
     centred, scale = norm_parts(dot(hidden, wn_out_ref[...]))
-    out_ref[...] = (nodes_ref[0:TOP, :].astype(F32) + centred * scale).astype(BF16)
+    top_ref[...] = (nodes_ref[0:TOP, :].astype(F32) + centred * scale).astype(BF16)
+    top = pltpu.make_async_copy(top_ref, out_hbm.at[pl.ds(0, TOP)], sems.at[1])
+    top.start()
+    rest.wait()
+    top.wait()
 
 
 def in_hbm(*arrays):
@@ -257,27 +255,35 @@
     (heads,) = call(
         head_kernel, "head", (blocks,), in_hbm(node_latents), hbm=(0,), scratch=[vmem((TOP, width), BF16), dma(())],
     )
-    lat = lax.all_to_all(heads, GROUP_AXES, 0, 0, axis_index_groups=[first_order(group)])
-    nodes, cedges, w_ends, w_out, to_even, to_odd, gather, picks, coarse_part = call(
+    lat = lax.all_to_all(heads, GROUP_AXES, 0, 0, axis_index_groups=[order(group)])
+    send, recv = ids(fine_senders), ids(fine_receivers)
+    nodes, cedges, w_self, w_ends, w_out, edges, send, recv, to_even, to_odd, gather, picks, coarse_part = call(
         load_kernel,
         "load",
         (
             like(node_latents),
             like(coarse_edges),
+            shape((width, width), BF16),
             shape((2 * width, width), BF16),
             like(w_edge_out),
+            like(edge_latents),
+            like(send),
+            like(recv),
             shape((halo, width), BF16),
             shape((halo, width), BF16),
             shape((2 * cedge_count, coarse_count), BF16),
             shape((coarse_count, cedge_count), BF16),
             shape((cedge_count, width), F32),
         ),
-        in_hbm(node_latents, halo_lists, coarse_edges, w_edge_in, ids(coarse_senders), ids(coarse_receivers), w_edge_out)
+        in_hbm(
+            node_latents, halo_lists, coarse_edges, w_edge_in, ids(coarse_senders), ids(coarse_receivers), w_edge_out,
+            edge_latents, send, recv,
+        )
         + [heads],
-        hbm=range(8),
+        hbm=range(11),
         scratch=[
-            vmem(halo_lists.shape, jnp.int32), vmem((width, width), BF16),
-            vmem((1, cedge_count), jnp.int32), vmem((1, cedge_count), jnp.int32), dma((8,)),
+            vmem(halo_lists.shape, jnp.int32), vmem((1, cedge_count), jnp.int32), vmem((1, cedge_count), jnp.int32),
+            dma((11,)),
         ],
         flops=edge_count * square,
     )
@@ -287,7 +293,7 @@
         [lat, cedges, coarse_part, gather, picks, w_ends, w_out], out_specs=[VMEM, ANY],
         scratch=[vmem(blocks.shape, BF16), dma(())],
     )
-    got = lax.all_to_all(sums, GROUP_AXES, 0, 0, axis_index_groups=[second_order(group)])
+    got = lax.all_to_all(sums, GROUP_AXES, 0, 0, axis_index_groups=[order(group)])
     new_edges, new_coarse, rest, agg, node_part, wn_agg, wn_out = call(
         fine_kernel,
         "fine",
@@ -300,28 +306,20 @@
             shape((width, width), BF16),
             like(w_node_out),
         ),
-        [from_even, nodes, from_odd, w_ends, w_out, new_coarse]
-        + in_hbm(edge_latents, w_edge_in, ids(fine_senders), ids(fine_receivers), w_node_in, w_node_out)
+        [from_even, nodes, from_odd, w_self, w_ends, w_out, edges, send, recv, new_coarse]
+        + in_hbm(w_node_in, w_node_out)
         + [sums],
-        hbm=range(6, 13),
+        hbm=range(10, 13),
         out_specs=[ANY] * 2 + [VMEM] * 5,
         scratch=[
-            vmem(edge_latents.shape, BF16), vmem((width, width), BF16), vmem((1, edge_count), jnp.int32),
-            vmem((1, edge_count), jnp.int32), vmem((width, width), BF16), vmem(edge_latents.shape, BF16), dma((7,)),
-            dma((edge_count // STEP + 1,)),
+            vmem((width, width), BF16), vmem(edge_latents.shape, BF16), dma((3,)), dma((edge_count // STEP + 1,)),
         ],
         flops=64 * edge_count * square,
     )
-    new_nodes = pl.pallas_call(
-        top_kernel,
-        grid=(1,),
-        out_shape=like(node_latents),
-        in_specs=[VMEM] * 6 + [ANY],
-        out_specs=pl.BlockSpec((TOP, width), lambda i: (0, 0)),
-        input_output_aliases={6: 0},
-        compiler_params=pltpu.CompilerParams(vmem_limit_bytes=16 * MIB),
-        name="top",
-    )(got, agg, node_part, nodes, wn_agg, wn_out, rest)
+    (new_nodes,) = call(
+        top_kernel, "top", (like(node_latents),), [got, agg, node_part, nodes, wn_agg, wn_out, rest], out_specs=[ANY],
+        scratch=[vmem((TOP, width), BF16), dma((2,))],
+    )
     return (new_nodes, new_edges, new_coarse)
 
 

time: 27.6 us -> 33.9 us (1.23)
  local copies, waits for them, and re-layouts: 0 us -> 5.72 us
  starting transfers between devices: 15.6 us -> 16.8 us
  Pallas kernels: 10.5 us -> 10 us
    unnamed x0 -> x20, local copies, waits for them, and re-layouts: none -> 5.72 us
    all_to_all x2, starting transfers between devices: 14.9 us -> 16.1 us  [the longest x1 8.84 us: body(): lax.all_to_all(heads, GROUP_AXES, 0, 0, axis_index_groups=[order(group)])]
    pallas_call x1 -> x0, Pallas kernels: 1.13 us -> none  [body(): pl.pallas_call(top_kernel, grid=(1,), out_shape=like(node_latents), in_sp...]
    pallas_call x4 -> x5, Pallas kernels: 9.4 us -> 10 us  [call(): pl.pallas_call(kernel, out_shape=outs, in_specs=[ANY if i in hbm else VME...]
  transfers between devices with their start and end apart: 4 -> 4, of which waited for: 1 -> 0; matrix products, arithmetic and copies ran while one was open for 0% -> 0% of each run, Pallas kernels for 30% -> 23%
where the time goes in v1:
time: 33.9 us; the launch traced here: 33.3 us
  starting transfers between devices  16.8 us (50%)
  Pallas kernels  10 us (29%)
  local copies, waits for them, and re-layouts  5.72 us (17%)
  between operations  0.72 us (2%)
    pallas_call x5, Pallas kernels, call(): pl.pallas_call(kernel, out_shape=outs, in_specs=[ANY if i in hbm else VME...  10 us
    all_to_all x1, starting transfers between devices, body(): lax.all_to_all(heads, GROUP_AXES, 0, 0, axis_index_groups=[order(group)])  8.84 us
    all_to_all x1, starting transfers between devices, body(): lax.all_to_all(sums, GROUP_AXES, 0, 0, axis_index_groups=[order(group)])  7.26 us
    unnamed x20, local copies, waits for them, and re-layouts  5.72 us
    ppermute x2, starting transfers between devices, pair(): return lax.ppermute(value, GROUP_AXES, pairs + [(b, a) for a, b in pairs])  0.69 us
  transfers between devices with their start and end apart: 4, of which 0 were waited for; matrix products, arithmetic and copies ran while one was open for 0% of the time, Pallas kernels for 23%

profile of v1, /device:TPU:0, one launch (start us, length us, event | category | flops | bytes accessed | tf_op | source)
XLA Modules:
  0.0 33.3 jit_solution(6129574831836666903)
XLA Ops:
  0.6 1.4 %head.1.after = bf16[16,4,512]{2,1,0:T(4,128)(2,1)} custom-call(bf16[128,512]{1,0:T(8,128)(2,1)} %nodes_hbm.3), custom_call_target="tpu_custom_call" | custom-call | tf_op jit(solution)/shard_map/head/pallas_call | solution.py:214
  2.0 8.8 %all-to-all-start = ((bf16[16,4,512]{2,1,0:T(4,128)(2,1)}), bf16[16,4,512]{2,1,0:T(4,128)(2,1)S(1)}, u32[]{:S(2)}, u32[]{:S(2)}) async-start(bf16[16,4,512]{2,1,0:T(4,128)(2,1)} %head.1.after), calls=%async_computation | async-start | bytes 131072 | tf_op jit(solution)/shard_map/all_to_all | solution.py:258
  10.8 1.9 %load.1 = (bf16[128,512]{1,0:T(8,128)(2,1)S(1)}, bf16[64,512]{1,0:T(8,128)(2,1)S(1)}, bf16[512,512]{1,0:T(8,128)(2,1)S(1)}, bf16[1024,512]{1,0:T(8,128)(2,1)S(1)...) custom-call(bf16[128,512]{1,0:T(8,128)(2,1)} %nodes_hbm.3, ...), custom_call_target="tpu_custom_call" | custom-call | flops 268435456 | tf_op jit(solution)/shard_map/load/pallas_call | solution.py:214
  12.8 0.0 copy-start.6
  12.8 0.6 %copy-done.6 = s32[1,512]{1,0:T(1,128)} copy-done((s32[1,512]{1,0:T(1,128)}, s32[1,512]{1,0:T(1,128)S(1)}, u32[]{:S(2)}) %copy-start.6) | copy-done | bytes 2072
  13.4 0.0 copy-start.8
  13.4 0.6 %copy-done.8 = s32[1,512]{1,0:T(1,128)} copy-done((s32[1,512]{1,0:T(1,128)}, s32[1,512]{1,0:T(1,128)S(1)}, u32[]{:S(2)}) %copy-start.8) | copy-done | bytes 2072
  14.0 0.0 copy-start
  14.0 0.1 collective-permute-start
  14.0 0.6 %collective-permute-start.1 = (bf16[16,512]{1,0:T(8,128)(2,1)S(1)}, bf16[16,512]{1,0:T(8,128)(2,1)S(1)}, u32[]{:S(2)}, u32[]{:S(2)}) collective-permute-start(bf16[16,512]{1,0:T(8,128)(2,1)S(1)} %get-tuple-element.34), channel_id=1, source_target_pairs={{1,2},{3,4},{5,6},{7,8},{9,10},{11,12},{13,14},{15,0},{2,1},{4,3},... | collective-permute-start | bytes 49160 | tf_op jit(solution)/shard_map/ppermute | solution.py:25
  14.6 0.0 all-to-all-done.lat_ref
  14.6 1.5 %coarse.1 = (bf16[64,512]{1,0:T(8,128)(2,1)S(1)}, bf16[16,4,512]{2,1,0:T(4,128)(2,1)}) custom-call(bf16[16,4,512]{2,1,0:T(4,128)(2,1)S(1)} %all-to-all-done.lat_ref, bf16[64,512]{1,0:T(8,128)(2,1)S(1)} %get-tuple-element.25.edges_ref, f32[64,512]{1,0:T(8,128)S(1)} %get-tuple-element.26.part_ref, bf16[128,64]{1,0:T(8,128)(2,1)S(1)} %get-tuple-element.27.gather_ref, ...), custom_call_target="tpu_custom_call" | custom-call | tf_op jit(solution)/shard_map/coarse/pallas_call | solution.py:214
  16.2 0.0 copy-start.2
  16.2 7.3 %all-to-all-start.1 = ((bf16[16,4,512]{2,1,0:T(4,128)(2,1)}), bf16[16,4,512]{2,1,0:T(4,128)(2,1)S(1)}, u32[]{:S(2)}, u32[]{:S(2)}) async-start(bf16[16,4,512]{2,1,0:T(4,128)(2,1)} %get-tuple-element.31.after), calls=%async_computation.1 | async-start | bytes 131072 | tf_op jit(solution)/shard_map/all_to_all | solution.py:296
  23.4 0.0 collective-permute-done.even_ref
  23.5 0.0 collective-permute-done.1.odd_ref
  23.5 0.0 copy-start.4
  23.5 0.6 %copy-done.4 = bf16[16,512]{1,0:T(8,128)(2,1)} copy-done((bf16[16,512]{1,0:T(8,128)(2,1)}, bf16[16,512]{1,0:T(8,128)(2,1)S(1)}, u32[]{:S(2)}) %copy-start.4) | copy-done | bytes 16408
  24.1 0.0 copy-done
  24.1 0.0 copy-done.2
  24.1 0.0 copy-start.1
  24.1 1.0 %copy-done.1 = bf16[512,512]{1,0:T(8,128)(2,1)S(1)} copy-done((bf16[512,512]{1,0:T(8,128)(2,1)S(1)}, bf16[512,512]{1,0:T(8,128)(2,1)}, u32[]{:S(2)}) %copy-start.1) | copy-done | bytes 524312
  25.1 0.0 copy-start.3
  25.1 0.8 %copy-done.3 = bf16[64,512]{1,0:T(8,128)(2,1)S(1)} copy-done((bf16[64,512]{1,0:T(8,128)(2,1)S(1)}, bf16[64,512]{1,0:T(8,128)(2,1)}, u32[]{:S(2)}) %copy-start.3) | copy-done | bytes 65560
  26.0 0.0 copy-start.5
  26.0 0.7 %copy-done.5 = bf16[16,512]{1,0:T(8,128)(2,1)S(1)} copy-done((bf16[16,512]{1,0:T(8,128)(2,1)S(1)}, bf16[16,512]{1,0:T(8,128)(2,1)}, u32[]{:S(2)}) %copy-start.5) | copy-done | bytes 16408
  26.7 0.0 copy-start.7
  26.7 0.7 %copy-done.7 = s32[1,512]{1,0:T(1,128)S(1)} copy-done((s32[1,512]{1,0:T(1,128)S(1)}, s32[1,512]{1,0:T(1,128)}, u32[]{:S(2)}) %copy-start.7) | copy-done | bytes 2072
  27.3 0.0 copy-start.9
  27.4 0.7 %copy-done.9 = s32[1,512]{1,0:T(1,128)S(1)} copy-done((s32[1,512]{1,0:T(1,128)S(1)}, s32[1,512]{1,0:T(1,128)}, u32[]{:S(2)}) %copy-start.9) | copy-done | bytes 2072
  28.0 4.1 %fine.1 = (bf16[512,512]{1,0:T(8,128)(2,1)}, bf16[64,512]{1,0:T(8,128)(2,1)}, bf16[128,512]{1,0:T(8,128)(2,1)S(1)}, f32[16,512]{1,0:T(8,128)S(1)}, f32[16,512]{1...) custom-call(bf16[16,512]{1,0:T(8,128)(2,1)S(1)} %collective-permute-done.even_ref, ...), custom_call_target="tpu_custom_call" | custom-call | flops 17179869184 | tf_op jit(solution)/shard_map/fine/pallas_call | solution.py:214
  32.1 0.0 all-to-all-done.1.got_ref
  32.1 1.1 %top.1 = bf16[128,512]{1,0:T(8,128)(2,1)} custom-call(bf16[16,4,512]{2,1,0:T(4,128)(2,1)S(1)} %all-to-all-done.1.got_ref, f32[16,512]{1,0:T(8,128)S(1)} %get-tuple-element.40.agg_ref, f32[16,512]{1,0:T(8,128)S(1)} %get-tuple-element.41.part_ref, bf16[128,512]{1,0:T(8,128)(2,1)S(1)} %get-tuple-element.33.nodes_ref, ...), custom_call_target="tpu_custom_call" | custom-call | tf_op jit(solution)/shard_map/top/pallas_call | solution.py:214
Async XLA Ops:
  2.0 12.6 %all-to-all-start = ((bf16[16,4,512]{2,1,0:T(4,128)(2,1)}), bf16[16,4,512]{2,1,0:T(4,128)(2,1)S(1)}, u32[]{:S(2)}, u32[]{:S(2)}) async-start(bf16[16,4,512]{2,1,0:T(4,128)(2,1)} %head.1.after), calls=%async_computation | async-start | bytes 131072 | tf_op jit(solution)/shard_map/all_to_all | solution.py:258
  12.8 0.6 %copy-start.6 = (s32[1,512]{1,0:T(1,128)}, s32[1,512]{1,0:T(1,128)S(1)}, u32[]{:S(2)}) copy-start(s32[1,512]{1,0:T(1,128)S(1)} %get-tuple-element.37.send_ref) | copy-start | bytes 6148
  13.4 0.6 %copy-start.8 = (s32[1,512]{1,0:T(1,128)}, s32[1,512]{1,0:T(1,128)S(1)}, u32[]{:S(2)}) copy-start(s32[1,512]{1,0:T(1,128)S(1)} %get-tuple-element.38.recv_ref) | copy-start | bytes 6148
  14.0 10.1 %copy-start = (bf16[512,512]{1,0:T(8,128)(2,1)}, bf16[512,512]{1,0:T(8,128)(2,1)S(1)}, u32[]{:S(2)}) copy-start(bf16[512,512]{1,0:T(8,128)(2,1)S(1)} %get-tuple-element.36.edges_ref) | copy-start | bytes 1572868
  14.0 9.5 %collective-permute-start = (bf16[16,512]{1,0:T(8,128)(2,1)S(1)}, bf16[16,512]{1,0:T(8,128)(2,1)S(1)}, u32[]{:S(2)}, u32[]{:S(2)}) collective-permute-start(bf16[16,512]{1,0:T(8,128)(2,1)S(1)} %get-tuple-element.32), channel_id=1, source_target_pairs={{0,1},{2,3},{4,5},{6,7},{8,9},{10,11},{12,13},{14,15},{1,0},{3,2},... | collective-permute-start | bytes 49160 | tf_op jit(solution)/shard_map/ppermute | solution.py:25
  14.0 9.4 %collective-permute-start.1 = (bf16[16,512]{1,0:T(8,128)(2,1)S(1)}, bf16[16,512]{1,0:T(8,128)(2,1)S(1)}, u32[]{:S(2)}, u32[]{:S(2)}) collective-permute-start(bf16[16,512]{1,0:T(8,128)(2,1)S(1)} %get-tuple-element.34), channel_id=1, source_target_pairs={{1,2},{3,4},{5,6},{7,8},{9,10},{11,12},{13,14},{15,0},{2,1},{4,3},... | collective-permute-start | bytes 49160 | tf_op jit(solution)/shard_map/ppermute | solution.py:25
  16.2 7.9 %copy-start.2 = (bf16[64,512]{1,0:T(8,128)(2,1)}, bf16[64,512]{1,0:T(8,128)(2,1)S(1)}, u32[]{:S(2)}) copy-start(bf16[64,512]{1,0:T(8,128)(2,1)S(1)} %get-tuple-element.39.coarse_ref) | copy-start | bytes 196612
  16.2 16.0 %all-to-all-start.1 = ((bf16[16,4,512]{2,1,0:T(4,128)(2,1)}), bf16[16,4,512]{2,1,0:T(4,128)(2,1)S(1)}, u32[]{:S(2)}, u32[]{:S(2)}) async-start(bf16[16,4,512]{2,1,0:T(4,128)(2,1)} %get-tuple-element.31.after), calls=%async_computation.1 | async-start | bytes 131072 | tf_op jit(solution)/shard_map/all_to_all | solution.py:296
  23.5 0.6 %copy-start.4 = (bf16[16,512]{1,0:T(8,128)(2,1)}, bf16[16,512]{1,0:T(8,128)(2,1)S(1)}, u32[]{:S(2)}) copy-start(bf16[16,512]{1,0:T(8,128)(2,1)S(1)} %collective-permute-done.1.odd_ref) | copy-start | bytes 49156
  24.1 1.0 %copy-start.1 = (bf16[512,512]{1,0:T(8,128)(2,1)S(1)}, bf16[512,512]{1,0:T(8,128)(2,1)}, u32[]{:S(2)}) copy-start(bf16[512,512]{1,0:T(8,128)(2,1)} %copy-done) | copy-start | bytes 1572868
  25.1 0.8 %copy-start.3 = (bf16[64,512]{1,0:T(8,128)(2,1)S(1)}, bf16[64,512]{1,0:T(8,128)(2,1)}, u32[]{:S(2)}) copy-start(bf16[64,512]{1,0:T(8,128)(2,1)} %copy-done.2) | copy-start | bytes 196612
  26.0 0.7 %copy-start.5 = (bf16[16,512]{1,0:T(8,128)(2,1)S(1)}, bf16[16,512]{1,0:T(8,128)(2,1)}, u32[]{:S(2)}) copy-start(bf16[16,512]{1,0:T(8,128)(2,1)} %copy-done.4) | copy-start | bytes 49156
  26.7 0.7 %copy-start.7 = (s32[1,512]{1,0:T(1,128)S(1)}, s32[1,512]{1,0:T(1,128)}, u32[]{:S(2)}) copy-start(s32[1,512]{1,0:T(1,128)} %copy-done.6) | copy-start | bytes 6148
  27.3 0.7 %copy-start.9 = (s32[1,512]{1,0:T(1,128)S(1)}, s32[1,512]{1,0:T(1,128)}, u32[]{:S(2)}) copy-start(s32[1,512]{1,0:T(1,128)} %copy-done.8) | copy-start | bytes 6148

commit v2 on v1

--- a/solution.py
+++ b/solution.py
@@ -8,15 +8,16 @@
 CO_DEV = 4
 GROUP_AXES = ("patch", "sub")
 TOP = 16
-STEP = 256
+STEP = 512
 MIB = 1 << 20
+FIRST, SECOND = 2, 3
 ANY = pl.BlockSpec(memory_space=pl.ANY)
 VMEM = pl.BlockSpec(memory_space=pltpu.VMEM)
 BF16, F32 = jnp.bfloat16, jnp.float32
 
 
-def order(group):
-    return list(reversed(range(group)))
+def order(group, quarter):
+    return [(i + group * quarter // 4) % group for i in range(group)]
 
 
 def pair(value, first):
@@ -66,20 +67,19 @@
 
 
 def load_kernel(
-    nodes_hbm, lists_hbm, cedges_hbm, w_in_hbm, csend_hbm, crecv_hbm, w_out_hbm, edges_hbm, send_hbm, recv_hbm, after,
-    nodes_ref, cedges_ref, w_self_ref, w_ends_ref, w_out_ref, edges_ref, send_ref, recv_ref,
+    nodes_hbm, lists_hbm, cedges_hbm, w_in_hbm, csend_hbm, crecv_hbm, w_out_hbm, send_hbm, recv_hbm, after,
+    nodes_ref, cedges_ref, w_ends_ref, w_out_ref, send_ref, recv_ref,
     even_ref, odd_ref, gather_ref, picks_ref, part_ref,
-    lists_ref, csend_ref, crecv_ref, sems,
+    lists_ref, w_self_ref, csend_ref, crecv_ref, sems,
 ):
     width = nodes_ref.shape[1]
     copies = start_copies(
         [
             nodes_hbm, lists_hbm, cedges_hbm, w_in_hbm.at[pl.ds(0, width)], csend_hbm, crecv_hbm,
-            w_in_hbm.at[pl.ds(width, 2 * width)], w_out_hbm, edges_hbm, send_hbm, recv_hbm,
+            w_in_hbm.at[pl.ds(width, 2 * width)], w_out_hbm, send_hbm, recv_hbm,
         ],
         [
-            nodes_ref, lists_ref, cedges_ref, w_self_ref, csend_ref, crecv_ref, w_ends_ref, w_out_ref, edges_ref,
-            send_ref, recv_ref,
+            nodes_ref, lists_ref, cedges_ref, w_self_ref, csend_ref, crecv_ref, w_ends_ref, w_out_ref, send_ref, recv_ref,
         ],
         sems,
     )
@@ -99,7 +99,7 @@
     part_ref[...] = dot(cedges_ref[...], w_self_ref[...])
     rows, ids = picks_ref.shape
     at = lax.broadcasted_iota(jnp.int32, (rows, ids), 0)
-    node = (rows // CO_DEV - 1 - at // CO_DEV) * CO_DEV + at % CO_DEV
+    node = (at + CO_DEV * order(rows // CO_DEV, FIRST)[0]) % rows
     send = jnp.where(node == csend_ref[...], 1.0, 0.0).astype(BF16)
     recv = jnp.where(node == crecv_ref[...], 1.0, 0.0).astype(BF16)
     picks_ref[...] = onehot_t(rows, crecv_ref[...])
@@ -124,7 +124,7 @@
     new = (edges_ref[...].astype(F32) + centred * scale).astype(BF16)
     new_ref[...] = new
     sums = dot(picks_ref[...], new).astype(BF16)
-    for at, owner in enumerate(order(blocks)):
+    for at, owner in enumerate(order(blocks, SECOND)):
         sums_ref[at] = sums[owner * CO_DEV : (owner + 1) * CO_DEV, :]
     copy = pltpu.make_async_copy(sums_ref, sums_hbm, sem)
     copy.start()
@@ -132,16 +132,19 @@
 
 
 def fine_kernel(
-    even_ref, nodes_ref, odd_ref, w_self_ref, w_ends_ref, w_out_ref, edges_ref, send_ref, recv_ref, coarse_ref,
-    wn_in_hbm, wn_out_hbm, after,
+    even_ref, nodes_ref, odd_ref, w_ends_ref, w_out_ref, send_ref, recv_ref, coarse_ref,
+    edges_hbm, w_in_hbm, wn_in_hbm, wn_out_hbm, after,
     new_hbm, coarse_hbm, out_ref, agg_ref, npart_ref, wn_agg_ref, wn_out_ref,
-    wn_self_ref, new_ref, sems, out_sems,
+    edges_ref, w_self_ref, wn_self_ref, new_ref, sems, out_sems,
 ):
     nodes = nodes_ref[...]
     count, width = nodes.shape
     copies = start_copies(
-        [wn_in_hbm.at[pl.ds(0, width)], wn_in_hbm.at[pl.ds(width, width)], wn_out_hbm],
-        [wn_self_ref, wn_agg_ref, wn_out_ref],
+        [
+            edges_hbm, w_in_hbm.at[pl.ds(0, width)],
+            wn_in_hbm.at[pl.ds(0, width)], wn_in_hbm.at[pl.ds(width, width)], wn_out_hbm,
+        ],
+        [edges_ref, w_self_ref, wn_self_ref, wn_agg_ref, wn_out_ref],
         sems,
     )
     outs = [pltpu.make_async_copy(coarse_ref, coarse_hbm, out_sems.at[0])]
@@ -159,8 +162,12 @@
         senders = dot_t(onehot_t(extended.shape[0], send_ref[:, rows]), extended).astype(BF16)
         receivers = dot_t(picks, nodes).astype(BF16)
         valid = dot_t(picks, ones)[:, 0:1]
+        pre = dot(jnp.concatenate([senders, receivers], axis=1), w_ends_ref[...])
+        if at == 0:
+            for copy in copies[:2]:
+                copy.wait()
         edges = edges_ref[rows, :]
-        pre = dot(edges, w_self_ref[...]) + dot(jnp.concatenate([senders, receivers], axis=1), w_ends_ref[...])
+        pre = pre + dot(edges, w_self_ref[...])
         hidden = silu(pre).astype(BF16)
         centred, scale = norm_parts(dot(hidden, w_out_ref[...]))
         new = (edges.astype(F32) + centred * (scale * valid)).astype(BF16)
@@ -170,7 +177,7 @@
         outs.append(copy)
         total = total + dot(picks, new)
     agg_ref[...] = total[0:TOP]
-    for copy in copies:
+    for copy in copies[2:]:
         copy.wait()
     pre = dot(nodes, wn_self_ref[...])
     npart_ref[...] = pre[0:TOP]
@@ -255,18 +262,16 @@
     (heads,) = call(
         head_kernel, "head", (blocks,), in_hbm(node_latents), hbm=(0,), scratch=[vmem((TOP, width), BF16), dma(())],
     )
-    lat = lax.all_to_all(heads, GROUP_AXES, 0, 0, axis_index_groups=[order(group)])
+    lat = lax.all_to_all(heads, GROUP_AXES, 0, 0, axis_index_groups=[order(group, FIRST)])
     send, recv = ids(fine_senders), ids(fine_receivers)
-    nodes, cedges, w_self, w_ends, w_out, edges, send, recv, to_even, to_odd, gather, picks, coarse_part = call(
+    nodes, cedges, w_ends, w_out, send, recv, to_even, to_odd, gather, picks, coarse_part = call(
         load_kernel,
         "load",
         (
             like(node_latents),
             like(coarse_edges),
-            shape((width, width), BF16),
             shape((2 * width, width), BF16),
             like(w_edge_out),
-            like(edge_latents),
             like(send),
             like(recv),
             shape((halo, width), BF16),
@@ -277,13 +282,13 @@
         ),
         in_hbm(
             node_latents, halo_lists, coarse_edges, w_edge_in, ids(coarse_senders), ids(coarse_receivers), w_edge_out,
-            edge_latents, send, recv,
+            send, recv,
         )
         + [heads],
-        hbm=range(11),
+        hbm=range(10),
         scratch=[
-            vmem(halo_lists.shape, jnp.int32), vmem((1, cedge_count), jnp.int32), vmem((1, cedge_count), jnp.int32),
-            dma((11,)),
+            vmem(halo_lists.shape, jnp.int32), vmem((width, width), BF16),
+            vmem((1, cedge_count), jnp.int32), vmem((1, cedge_count), jnp.int32), dma((10,)),
         ],
         flops=edge_count * square,
     )
@@ -293,7 +298,7 @@
         [lat, cedges, coarse_part, gather, picks, w_ends, w_out], out_specs=[VMEM, ANY],
         scratch=[vmem(blocks.shape, BF16), dma(())],
     )
-    got = lax.all_to_all(sums, GROUP_AXES, 0, 0, axis_index_groups=[order(group)])
+    got = lax.all_to_all(sums, GROUP_AXES, 0, 0, axis_index_groups=[order(group, SECOND)])
     new_edges, new_coarse, rest, agg, node_part, wn_agg, wn_out = call(
         fine_kernel,
         "fine",
@@ -306,13 +311,14 @@
             shape((width, width), BF16),
             like(w_node_out),
         ),
-        [from_even, nodes, from_odd, w_self, w_ends, w_out, edges, send, recv, new_coarse]
-        + in_hbm(w_node_in, w_node_out)
+        [from_even, nodes, from_odd, w_ends, w_out, send, recv, new_coarse]
+        + in_hbm(edge_latents, w_edge_in, w_node_in, w_node_out)
         + [sums],
-        hbm=range(10, 13),
+        hbm=range(8, 13),
         out_specs=[ANY] * 2 + [VMEM] * 5,
         scratch=[
-            vmem((width, width), BF16), vmem(edge_latents.shape, BF16), dma((3,)), dma((edge_count // STEP + 1,)),
+            vmem(edge_latents.shape, BF16), vmem((width, width), BF16), vmem((width, width), BF16),
+            vmem(edge_latents.shape, BF16), dma((5,)), dma((edge_count // STEP + 1,)),
         ],
         flops=64 * edge_count * square,
     )

time: 33.9 us -> 27 us (0.80)
  local copies, waits for them, and re-layouts: 5.72 us -> 0 us
  starting transfers between devices: 16.8 us -> 15.7 us
    unnamed x20 -> x0, local copies, waits for them, and re-layouts: 5.72 us -> none
    all_to_all x2, starting transfers between devices: 16.1 us -> 13.2 us  [the longest x1 7.84 us: body(): lax.all_to_all(heads, GROUP_AXES, 0, 0, axis_index_groups=[order(group, F...]
    ppermute x2, starting transfers between devices: 0.69 us -> 2.54 us  [pair(): return lax.ppermute(value, GROUP_AXES, pairs + [(b, a) for a, b in pairs])]
  transfers between devices with their start and end apart: 4 -> 4, of which waited for: 0 -> 1; matrix products, arithmetic and copies ran while one was open for 0% -> 0% of each run, Pallas kernels for 23% -> 28%
where the time goes in v2:
time: 27 us; the launch traced here: 26.6 us
  starting transfers between devices  15.7 us (58%)
  Pallas kernels  9.85 us (36%)
  between operations  0.68 us (3%)
  waiting for transfers between devices  0.33 us (1%)
    pallas_call x5, Pallas kernels, call(): pl.pallas_call(kernel, out_shape=outs, in_specs=[ANY if i in hbm else VME...  9.85 us
    all_to_all x1, starting transfers between devices, body(): lax.all_to_all(heads, GROUP_AXES, 0, 0, axis_index_groups=[order(group, F...  7.84 us
    all_to_all x1, starting transfers between devices, body(): lax.all_to_all(sums, GROUP_AXES, 0, 0, axis_index_groups=[order(group, SE...  5.34 us
    ppermute x2, starting transfers between devices, pair(): return lax.ppermute(value, GROUP_AXES, pairs + [(b, a) for a, b in pairs])  2.54 us
  transfers between devices with their start and end apart: 4, of which 1 were waited for; matrix products, arithmetic and copies ran while one was open for 0% of the time, Pallas kernels for 28%

profile of v2, /device:TPU:0, one launch (start us, length us, event | category | flops | bytes accessed | tf_op | source)
XLA Modules:
  0.0 26.6 jit_solution(7637934272936873855)
XLA Ops:
  0.6 1.4 %head.1.after = bf16[16,4,512]{2,1,0:T(4,128)(2,1)} custom-call(bf16[128,512]{1,0:T(8,128)(2,1)} %nodes_hbm.3), custom_call_target="tpu_custom_call" | custom-call | tf_op jit(solution)/shard_map/head/pallas_call | solution.py:221
  2.0 7.8 %all-to-all-start = ((bf16[16,4,512]{2,1,0:T(4,128)(2,1)}), bf16[16,4,512]{2,1,0:T(4,128)(2,1)S(1)}, u32[]{:S(2)}, u32[]{:S(2)}) async-start(bf16[16,4,512]{2,1,0:T(4,128)(2,1)} %head.1.after), calls=%async_computation | async-start | bytes 131072 | tf_op jit(solution)/shard_map/all_to_all | solution.py:265
  9.8 1.8 %load.1 = (bf16[128,512]{1,0:T(8,128)(2,1)S(1)}, bf16[64,512]{1,0:T(8,128)(2,1)S(1)}, bf16[1024,512]{1,0:T(8,128)(2,1)S(1)}, bf16[512,512]{1,0:T(8,128)(2,1)S(1)...) custom-call(bf16[128,512]{1,0:T(8,128)(2,1)} %nodes_hbm.3, ...), custom_call_target="tpu_custom_call" | custom-call | flops 268435456 | tf_op jit(solution)/shard_map/load/pallas_call | solution.py:221
  11.6 0.2 collective-permute-start
  11.8 2.3 %collective-permute-start.1 = (bf16[16,512]{1,0:T(8,128)(2,1)S(1)}, bf16[16,512]{1,0:T(8,128)(2,1)S(1)}, u32[]{:S(2)}, u32[]{:S(2)}) collective-permute-start(bf16[16,512]{1,0:T(8,128)(2,1)S(1)} %get-tuple-element.32), channel_id=1, source_target_pairs={{1,2},{3,4},{5,6},{7,8},{9,10},{11,12},{13,14},{15,0},{2,1},{4,3},... | collective-permute-start | bytes 49160 | tf_op jit(solution)/shard_map/ppermute | solution.py:26
  14.2 0.3 %all-to-all-done.lat_ref = bf16[16,4,512]{2,1,0:T(4,128)(2,1)S(1)} async-done(((bf16[16,4,512]{2,1,0:T(4,128)(2,1)}), bf16[16,4,512]{2,1,0:T(4,128)(2,1)S(1)}, u32[]{:S(2)}, u32[]{:S(2)}) %all-to-all-start) | async-done | bytes 65568 | tf_op jit(solution)/shard_map/all_to_all | solution.py:265
  14.5 1.5 %coarse.1 = (bf16[64,512]{1,0:T(8,128)(2,1)S(1)}, bf16[16,4,512]{2,1,0:T(4,128)(2,1)}) custom-call(bf16[16,4,512]{2,1,0:T(4,128)(2,1)S(1)} %all-to-all-done.lat_ref, bf16[64,512]{1,0:T(8,128)(2,1)S(1)} %get-tuple-element.23.edges_ref, f32[64,512]{1,0:T(8,128)S(1)} %get-tuple-element.24.part_ref, bf16[128,64]{1,0:T(8,128)(2,1)S(1)} %get-tuple-element.25.gather_ref, ...), custom_call_target="tpu_custom_call" | custom-call | tf_op jit(solution)/shard_map/coarse/pallas_call | solution.py:221
  16.0 5.3 %all-to-all-start.1 = ((bf16[16,4,512]{2,1,0:T(4,128)(2,1)}), bf16[16,4,512]{2,1,0:T(4,128)(2,1)S(1)}, u32[]{:S(2)}, u32[]{:S(2)}) async-start(bf16[16,4,512]{2,1,0:T(4,128)(2,1)} %get-tuple-element.29.after), calls=%async_computation.1 | async-start | bytes 131072 | tf_op jit(solution)/shard_map/all_to_all | solution.py:301
  21.3 0.0 collective-permute-done.even_ref
  21.3 0.0 collective-permute-done.1.odd_ref
  21.4 4.1 %fine.1 = (bf16[512,512]{1,0:T(8,128)(2,1)}, bf16[64,512]{1,0:T(8,128)(2,1)}, bf16[128,512]{1,0:T(8,128)(2,1)S(1)}, f32[16,512]{1,0:T(8,128)S(1)}, f32[16,512]{1...) custom-call(bf16[16,512]{1,0:T(8,128)(2,1)S(1)} %collective-permute-done.even_ref, ...), custom_call_target="tpu_custom_call" | custom-call | flops 17179869184 | tf_op jit(solution)/shard_map/fine/pallas_call | solution.py:221
  25.4 0.0 all-to-all-done.1.got_ref
  25.4 1.1 %top.1 = bf16[128,512]{1,0:T(8,128)(2,1)} custom-call(bf16[16,4,512]{2,1,0:T(4,128)(2,1)S(1)} %all-to-all-done.1.got_ref, f32[16,512]{1,0:T(8,128)S(1)} %get-tuple-element.36.agg_ref, f32[16,512]{1,0:T(8,128)S(1)} %get-tuple-element.37.part_ref, bf16[128,512]{1,0:T(8,128)(2,1)S(1)} %get-tuple-element.31.nodes_ref, ...), custom_call_target="tpu_custom_call" | custom-call | tf_op jit(solution)/shard_map/top/pallas_call | solution.py:221
Async XLA Ops:
  2.0 12.5 %all-to-all-start = ((bf16[16,4,512]{2,1,0:T(4,128)(2,1)}), bf16[16,4,512]{2,1,0:T(4,128)(2,1)S(1)}, u32[]{:S(2)}, u32[]{:S(2)}) async-start(bf16[16,4,512]{2,1,0:T(4,128)(2,1)} %head.1.after), calls=%async_computation | async-start | bytes 131072 | tf_op jit(solution)/shard_map/all_to_all | solution.py:265
  11.6 9.7 %collective-permute-start = (bf16[16,512]{1,0:T(8,128)(2,1)S(1)}, bf16[16,512]{1,0:T(8,128)(2,1)S(1)}, u32[]{:S(2)}, u32[]{:S(2)}) collective-permute-start(bf16[16,512]{1,0:T(8,128)(2,1)S(1)} %get-tuple-element.30), channel_id=1, source_target_pairs={{0,1},{2,3},{4,5},{6,7},{8,9},{10,11},{12,13},{14,15},{1,0},{3,2},... | collective-permute-start | bytes 49160 | tf_op jit(solution)/shard_map/ppermute | solution.py:26
  11.8 9.5 %collective-permute-start.1 = (bf16[16,512]{1,0:T(8,128)(2,1)S(1)}, bf16[16,512]{1,0:T(8,128)(2,1)S(1)}, u32[]{:S(2)}, u32[]{:S(2)}) collective-permute-start(bf16[16,512]{1,0:T(8,128)(2,1)S(1)} %get-tuple-element.32), channel_id=1, source_target_pairs={{1,2},{3,4},{5,6},{7,8},{9,10},{11,12},{13,14},{15,0},{2,1},{4,3},... | collective-permute-start | bytes 49160 | tf_op jit(solution)/shard_map/ppermute | solution.py:26
  16.0 9.4 %all-to-all-start.1 = ((bf16[16,4,512]{2,1,0:T(4,128)(2,1)}), bf16[16,4,512]{2,1,0:T(4,128)(2,1)S(1)}, u32[]{:S(2)}, u32[]{:S(2)}) async-start(bf16[16,4,512]{2,1,0:T(4,128)(2,1)} %get-tuple-element.29.after), calls=%async_computation.1 | async-start | bytes 131072 | tf_op jit(solution)/shard_map/all_to_all | solution.py:301

commit v3 on v2

--- a/solution.py
+++ b/solution.py
@@ -17,7 +17,7 @@
 
 
 def order(group, quarter):
-    return [(i + group * quarter // 4) % group for i in range(group)]
+    return [(group * quarter // 4 - i) % group for i in range(group)]
 
 
 def pair(value, first):
@@ -99,7 +99,8 @@
     part_ref[...] = dot(cedges_ref[...], w_self_ref[...])
     rows, ids = picks_ref.shape
     at = lax.broadcasted_iota(jnp.int32, (rows, ids), 0)
-    node = (at + CO_DEV * order(rows // CO_DEV, FIRST)[0]) % rows
+    count = rows // CO_DEV
+    node = (order(count, FIRST)[0] + count - at // CO_DEV) % count * CO_DEV + at % CO_DEV
     send = jnp.where(node == csend_ref[...], 1.0, 0.0).astype(BF16)
     recv = jnp.where(node == crecv_ref[...], 1.0, 0.0).astype(BF16)
     picks_ref[...] = onehot_t(rows, crecv_ref[...])

time: 27 us -> 27 us (level)
  starting transfers between devices: 15.7 us -> 16 us
  waiting for transfers between devices: 0.33 us -> 0.06 us
where the time goes in v3:
time: 27 us; the launch traced here: 26.6 us
  starting transfers between devices  16 us (59%)
  Pallas kernels  9.84 us (36%)
  between operations  0.68 us (3%)
    pallas_call x5, Pallas kernels, call(): pl.pallas_call(kernel, out_shape=outs, in_specs=[ANY if i in hbm else VME...  9.84 us
    all_to_all x1, starting transfers between devices, body(): lax.all_to_all(heads, GROUP_AXES, 0, 0, axis_index_groups=[order(group, F...  7.88 us
    all_to_all x1, starting transfers between devices, body(): lax.all_to_all(sums, GROUP_AXES, 0, 0, axis_index_groups=[order(group, SE...  5.59 us
    ppermute x2, starting transfers between devices, pair(): return lax.ppermute(value, GROUP_AXES, pairs + [(b, a) for a, b in pairs])  2.54 us
  transfers between devices with their start and end apart: 4, of which 1 were waited for; matrix products, arithmetic and copies ran while one was open for 0% of the time, Pallas kernels for 28%

profile of v3, /device:TPU:0, one launch (start us, length us, event | category | flops | bytes accessed | tf_op | source)
XLA Modules:
  0.0 26.6 jit_solution(17917189199593566357)
XLA Ops:
  0.6 1.4 %head.1.after = bf16[16,4,512]{2,1,0:T(4,128)(2,1)} custom-call(bf16[128,512]{1,0:T(8,128)(2,1)} %nodes_hbm.3), custom_call_target="tpu_custom_call" | custom-call | tf_op jit(solution)/shard_map/head/pallas_call | solution.py:222
  2.0 7.9 %all-to-all-start = ((bf16[16,4,512]{2,1,0:T(4,128)(2,1)}), bf16[16,4,512]{2,1,0:T(4,128)(2,1)S(1)}, u32[]{:S(2)}, u32[]{:S(2)}) async-start(bf16[16,4,512]{2,1,0:T(4,128)(2,1)} %head.1.after), calls=%async_computation | async-start | bytes 131072 | tf_op jit(solution)/shard_map/all_to_all | solution.py:266
  9.9 1.8 %load.1 = (bf16[128,512]{1,0:T(8,128)(2,1)S(1)}, bf16[64,512]{1,0:T(8,128)(2,1)S(1)}, bf16[1024,512]{1,0:T(8,128)(2,1)S(1)}, bf16[512,512]{1,0:T(8,128)(2,1)S(1)...) custom-call(bf16[128,512]{1,0:T(8,128)(2,1)} %nodes_hbm.3, ...), custom_call_target="tpu_custom_call" | custom-call | flops 268435456 | tf_op jit(solution)/shard_map/load/pallas_call | solution.py:222
  11.6 0.1 collective-permute-start
  11.8 2.4 %collective-permute-start.1 = (bf16[16,512]{1,0:T(8,128)(2,1)S(1)}, bf16[16,512]{1,0:T(8,128)(2,1)S(1)}, u32[]{:S(2)}, u32[]{:S(2)}) collective-permute-start(bf16[16,512]{1,0:T(8,128)(2,1)S(1)} %get-tuple-element.32), channel_id=1, source_target_pairs={{1,2},{3,4},{5,6},{7,8},{9,10},{11,12},{13,14},{15,0},{2,1},{4,3},... | collective-permute-start | bytes 49160 | tf_op jit(solution)/shard_map/ppermute | solution.py:26
  14.2 0.1 all-to-all-done.lat_ref
  14.2 1.5 %coarse.1 = (bf16[64,512]{1,0:T(8,128)(2,1)S(1)}, bf16[16,4,512]{2,1,0:T(4,128)(2,1)}) custom-call(bf16[16,4,512]{2,1,0:T(4,128)(2,1)S(1)} %all-to-all-done.lat_ref, bf16[64,512]{1,0:T(8,128)(2,1)S(1)} %get-tuple-element.23.edges_ref, f32[64,512]{1,0:T(8,128)S(1)} %get-tuple-element.24.part_ref, bf16[128,64]{1,0:T(8,128)(2,1)S(1)} %get-tuple-element.25.gather_ref, ...), custom_call_target="tpu_custom_call" | custom-call | tf_op jit(solution)/shard_map/coarse/pallas_call | solution.py:222
  15.8 5.6 %all-to-all-start.1 = ((bf16[16,4,512]{2,1,0:T(4,128)(2,1)}), bf16[16,4,512]{2,1,0:T(4,128)(2,1)S(1)}, u32[]{:S(2)}, u32[]{:S(2)}) async-start(bf16[16,4,512]{2,1,0:T(4,128)(2,1)} %get-tuple-element.29.after), calls=%async_computation.1 | async-start | bytes 131072 | tf_op jit(solution)/shard_map/all_to_all | solution.py:302
  21.4 0.0 collective-permute-done.even_ref
  21.4 0.0 collective-permute-done.1.odd_ref
  21.4 4.1 %fine.1 = (bf16[512,512]{1,0:T(8,128)(2,1)}, bf16[64,512]{1,0:T(8,128)(2,1)}, bf16[128,512]{1,0:T(8,128)(2,1)S(1)}, f32[16,512]{1,0:T(8,128)S(1)}, f32[16,512]{1...) custom-call(bf16[16,512]{1,0:T(8,128)(2,1)S(1)} %collective-permute-done.even_ref, ...), custom_call_target="tpu_custom_call" | custom-call | flops 17179869184 | tf_op jit(solution)/shard_map/fine/pallas_call | solution.py:222
  25.4 0.0 all-to-all-done.1.got_ref
  25.5 1.1 %top.1 = bf16[128,512]{1,0:T(8,128)(2,1)} custom-call(bf16[16,4,512]{2,1,0:T(4,128)(2,1)S(1)} %all-to-all-done.1.got_ref, f32[16,512]{1,0:T(8,128)S(1)} %get-tuple-element.36.agg_ref, f32[16,512]{1,0:T(8,128)S(1)} %get-tuple-element.37.part_ref, bf16[128,512]{1,0:T(8,128)(2,1)S(1)} %get-tuple-element.31.nodes_ref, ...), custom_call_target="tpu_custom_call" | custom-call | tf_op jit(solution)/shard_map/top/pallas_call | solution.py:222
Async XLA Ops:
  2.0 12.2 %all-to-all-start = ((bf16[16,4,512]{2,1,0:T(4,128)(2,1)}), bf16[16,4,512]{2,1,0:T(4,128)(2,1)S(1)}, u32[]{:S(2)}, u32[]{:S(2)}) async-start(bf16[16,4,512]{2,1,0:T(4,128)(2,1)} %head.1.after), calls=%async_computation | async-start | bytes 131072 | tf_op jit(solution)/shard_map/all_to_all | solution.py:266
  11.6 9.7 %collective-permute-start = (bf16[16,512]{1,0:T(8,128)(2,1)S(1)}, bf16[16,512]{1,0:T(8,128)(2,1)S(1)}, u32[]{:S(2)}, u32[]{:S(2)}) collective-permute-start(bf16[16,512]{1,0:T(8,128)(2,1)S(1)} %get-tuple-element.30), channel_id=1, source_target_pairs={{0,1},{2,3},{4,5},{6,7},{8,9},{10,11},{12,13},{14,15},{1,0},{3,2},... | collective-permute-start | bytes 49160 | tf_op jit(solution)/shard_map/ppermute | solution.py:26
  11.8 9.6 %collective-permute-start.1 = (bf16[16,512]{1,0:T(8,128)(2,1)S(1)}, bf16[16,512]{1,0:T(8,128)(2,1)S(1)}, u32[]{:S(2)}, u32[]{:S(2)}) collective-permute-start(bf16[16,512]{1,0:T(8,128)(2,1)S(1)} %get-tuple-element.32), channel_id=1, source_target_pairs={{1,2},{3,4},{5,6},{7,8},{9,10},{11,12},{13,14},{15,0},{2,1},{4,3},... | collective-permute-start | bytes 49160 | tf_op jit(solution)/shard_map/ppermute | solution.py:26
  15.8 9.7 %all-to-all-start.1 = ((bf16[16,4,512]{2,1,0:T(4,128)(2,1)}), bf16[16,4,512]{2,1,0:T(4,128)(2,1)S(1)}, u32[]{:S(2)}, u32[]{:S(2)}) async-start(bf16[16,4,512]{2,1,0:T(4,128)(2,1)} %get-tuple-element.29.after), calls=%async_computation.1 | async-start | bytes 131072 | tf_op jit(solution)/shard_map/all_to_all | solution.py:302

commit v4 on v2

--- a/solution.py
+++ b/solution.py
@@ -10,7 +10,7 @@
 TOP = 16
 STEP = 512
 MIB = 1 << 20
-FIRST, SECOND = 2, 3
+FIRST, SECOND = 2, 2
 ANY = pl.BlockSpec(memory_space=pl.ANY)
 VMEM = pl.BlockSpec(memory_space=pltpu.VMEM)
 BF16, F32 = jnp.bfloat16, jnp.float32

time: 27 us -> 26.5 us (0.981)
  starting transfers between devices: 15.7 us -> 14.8 us
  waiting for transfers between devices: 0.33 us -> 0.85 us
    all_to_all x1, starting transfers between devices: 5.34 us -> 4.38 us  [body(): lax.all_to_all(sums, GROUP_AXES, 0, 0, axis_index_groups=[order(group, SE...]
    all_to_all x1, waiting for transfers between devices: 0.01 us -> 0.53 us  [body(): lax.all_to_all(sums, GROUP_AXES, 0, 0, axis_index_groups=[order(group, SE...]
  transfers between devices with their start and end apart: 4 -> 4, of which waited for: 1 -> 2; matrix products, arithmetic and copies ran while one was open for 0% -> 0% of each run, Pallas kernels for 28% -> 28%
where the time goes in v4:
time: 26.5 us; the launch traced here: 26.1 us
  starting transfers between devices  14.8 us (56%)
  Pallas kernels  9.84 us (37%)
  waiting for transfers between devices  0.85 us (3%)
  between operations  0.68 us (3%)
    pallas_call x5, Pallas kernels, call(): pl.pallas_call(kernel, out_shape=outs, in_specs=[ANY if i in hbm else VME...  9.84 us
    all_to_all x1, starting transfers between devices, body(): lax.all_to_all(heads, GROUP_AXES, 0, 0, axis_index_groups=[order(group, F...  7.84 us
    all_to_all x1, starting transfers between devices, body(): lax.all_to_all(sums, GROUP_AXES, 0, 0, axis_index_groups=[order(group, SE...  4.38 us
    ppermute x2, starting transfers between devices, pair(): return lax.ppermute(value, GROUP_AXES, pairs + [(b, a) for a, b in pairs])  2.54 us
  transfers between devices with their start and end apart: 4, of which 2 were waited for; matrix products, arithmetic and copies ran while one was open for 0% of the time, Pallas kernels for 28%

profile of v4, /device:TPU:0, one launch (start us, length us, event | category | flops | bytes accessed | tf_op | source)
XLA Modules:
  0.0 26.1 jit_solution(9202356329128927949)
XLA Ops:
  0.6 1.4 %head.1.after = bf16[16,4,512]{2,1,0:T(4,128)(2,1)} custom-call(bf16[128,512]{1,0:T(8,128)(2,1)} %nodes_hbm.3), custom_call_target="tpu_custom_call" | custom-call | tf_op jit(solution)/shard_map/head/pallas_call | solution.py:221
  2.0 7.8 %all-to-all-start = ((bf16[16,4,512]{2,1,0:T(4,128)(2,1)}), bf16[16,4,512]{2,1,0:T(4,128)(2,1)S(1)}, u32[]{:S(2)}, u32[]{:S(2)}) async-start(bf16[16,4,512]{2,1,0:T(4,128)(2,1)} %head.1.after), calls=%async_computation | async-start | bytes 131072 | tf_op jit(solution)/shard_map/all_to_all | solution.py:265
  9.8 1.8 %load.1 = (bf16[128,512]{1,0:T(8,128)(2,1)S(1)}, bf16[64,512]{1,0:T(8,128)(2,1)S(1)}, bf16[1024,512]{1,0:T(8,128)(2,1)S(1)}, bf16[512,512]{1,0:T(8,128)(2,1)S(1)...) custom-call(bf16[128,512]{1,0:T(8,128)(2,1)} %nodes_hbm.3, ...), custom_call_target="tpu_custom_call" | custom-call | flops 268435456 | tf_op jit(solution)/shard_map/load/pallas_call | solution.py:221
  11.6 0.2 collective-permute-start
  11.8 2.3 %collective-permute-start.1 = (bf16[16,512]{1,0:T(8,128)(2,1)S(1)}, bf16[16,512]{1,0:T(8,128)(2,1)S(1)}, u32[]{:S(2)}, u32[]{:S(2)}) collective-permute-start(bf16[16,512]{1,0:T(8,128)(2,1)S(1)} %get-tuple-element.32), channel_id=1, source_target_pairs={{1,2},{3,4},{5,6},{7,8},{9,10},{11,12},{13,14},{15,0},{2,1},{4,3},... | collective-permute-start | bytes 49160 | tf_op jit(solution)/shard_map/ppermute | solution.py:26
  14.2 0.3 %all-to-all-done.lat_ref = bf16[16,4,512]{2,1,0:T(4,128)(2,1)S(1)} async-done(((bf16[16,4,512]{2,1,0:T(4,128)(2,1)}), bf16[16,4,512]{2,1,0:T(4,128)(2,1)S(1)}, u32[]{:S(2)}, u32[]{:S(2)}) %all-to-all-start) | async-done | bytes 65568 | tf_op jit(solution)/shard_map/all_to_all | solution.py:265
  14.5 1.5 %coarse.1 = (bf16[64,512]{1,0:T(8,128)(2,1)S(1)}, bf16[16,4,512]{2,1,0:T(4,128)(2,1)}) custom-call(bf16[16,4,512]{2,1,0:T(4,128)(2,1)S(1)} %all-to-all-done.lat_ref, bf16[64,512]{1,0:T(8,128)(2,1)S(1)} %get-tuple-element.23.edges_ref, f32[64,512]{1,0:T(8,128)S(1)} %get-tuple-element.24.part_ref, bf16[128,64]{1,0:T(8,128)(2,1)S(1)} %get-tuple-element.25.gather_ref, ...), custom_call_target="tpu_custom_call" | custom-call | tf_op jit(solution)/shard_map/coarse/pallas_call | solution.py:221
  16.0 4.4 %all-to-all-start.1 = ((bf16[16,4,512]{2,1,0:T(4,128)(2,1)}), bf16[16,4,512]{2,1,0:T(4,128)(2,1)S(1)}, u32[]{:S(2)}, u32[]{:S(2)}) async-start(bf16[16,4,512]{2,1,0:T(4,128)(2,1)} %get-tuple-element.29.after), calls=%async_computation.1 | async-start | bytes 131072 | tf_op jit(solution)/shard_map/all_to_all | solution.py:301
  20.4 0.0 collective-permute-done.even_ref
  20.4 0.0 collective-permute-done.1.odd_ref
  20.4 4.1 %fine.1 = (bf16[512,512]{1,0:T(8,128)(2,1)}, bf16[64,512]{1,0:T(8,128)(2,1)}, bf16[128,512]{1,0:T(8,128)(2,1)S(1)}, f32[16,512]{1,0:T(8,128)S(1)}, f32[16,512]{1...) custom-call(bf16[16,512]{1,0:T(8,128)(2,1)S(1)} %collective-permute-done.even_ref, ...), custom_call_target="tpu_custom_call" | custom-call | flops 17179869184 | tf_op jit(solution)/shard_map/fine/pallas_call | solution.py:221
  24.5 0.5 %all-to-all-done.1.got_ref = bf16[16,4,512]{2,1,0:T(4,128)(2,1)S(1)} async-done(((bf16[16,4,512]{2,1,0:T(4,128)(2,1)}), bf16[16,4,512]{2,1,0:T(4,128)(2,1)S(1)}, u32[]{:S(2)}, u32[]{:S(2)}) %all-to-all-start.1) | async-done | bytes 65568 | tf_op jit(solution)/shard_map/all_to_all | solution.py:301
  25.0 1.1 %top.1 = bf16[128,512]{1,0:T(8,128)(2,1)} custom-call(bf16[16,4,512]{2,1,0:T(4,128)(2,1)S(1)} %all-to-all-done.1.got_ref, f32[16,512]{1,0:T(8,128)S(1)} %get-tuple-element.36.agg_ref, f32[16,512]{1,0:T(8,128)S(1)} %get-tuple-element.37.part_ref, bf16[128,512]{1,0:T(8,128)(2,1)S(1)} %get-tuple-element.31.nodes_ref, ...), custom_call_target="tpu_custom_call" | custom-call | tf_op jit(solution)/shard_map/top/pallas_call | solution.py:221
Async XLA Ops:
  2.0 12.5 %all-to-all-start = ((bf16[16,4,512]{2,1,0:T(4,128)(2,1)}), bf16[16,4,512]{2,1,0:T(4,128)(2,1)S(1)}, u32[]{:S(2)}, u32[]{:S(2)}) async-start(bf16[16,4,512]{2,1,0:T(4,128)(2,1)} %head.1.after), calls=%async_computation | async-start | bytes 131072 | tf_op jit(solution)/shard_map/all_to_all | solution.py:265
  11.6 8.8 %collective-permute-start = (bf16[16,512]{1,0:T(8,128)(2,1)S(1)}, bf16[16,512]{1,0:T(8,128)(2,1)S(1)}, u32[]{:S(2)}, u32[]{:S(2)}) collective-permute-start(bf16[16,512]{1,0:T(8,128)(2,1)S(1)} %get-tuple-element.30), channel_id=1, source_target_pairs={{0,1},{2,3},{4,5},{6,7},{8,9},{10,11},{12,13},{14,15},{1,0},{3,2},... | collective-permute-start | bytes 49160 | tf_op jit(solution)/shard_map/ppermute | solution.py:26
  11.8 8.6 %collective-permute-start.1 = (bf16[16,512]{1,0:T(8,128)(2,1)S(1)}, bf16[16,512]{1,0:T(8,128)(2,1)S(1)}, u32[]{:S(2)}, u32[]{:S(2)}) collective-permute-start(bf16[16,512]{1,0:T(8,128)(2,1)S(1)} %get-tuple-element.32), channel_id=1, source_target_pairs={{1,2},{3,4},{5,6},{7,8},{9,10},{11,12},{13,14},{15,0},{2,1},{4,3},... | collective-permute-start | bytes 49160 | tf_op jit(solution)/shard_map/ppermute | solution.py:26
  16.0 9.0 %all-to-all-start.1 = ((bf16[16,4,512]{2,1,0:T(4,128)(2,1)}), bf16[16,4,512]{2,1,0:T(4,128)(2,1)S(1)}, u32[]{:S(2)}, u32[]{:S(2)}) async-start(bf16[16,4,512]{2,1,0:T(4,128)(2,1)} %get-tuple-element.29.after), calls=%async_computation.1 | async-start | bytes 131072 | tf_op jit(solution)/shard_map/all_to_all | solution.py:301

commit v5 on v4

--- a/solution.py
+++ b/solution.py
@@ -112,7 +112,7 @@
 
 
 def coarse_kernel(
-    lat_ref, edges_ref, part_ref, gather_ref, picks_ref, w_ends_ref, w_out_ref, new_ref, sums_hbm, sums_ref, sem
+    lat_ref, edges_ref, part_ref, gather_ref, picks_ref, w_ends_ref, w_out_ref, new_ref, sums_ref
 ):
     count, width = edges_ref.shape
     blocks = lat_ref.shape[0]
@@ -126,9 +126,6 @@
     sums = dot(picks_ref[...], new).astype(BF16)
     for at, owner in enumerate(order(blocks, SECOND)):
         sums_ref[at] = sums[owner * CO_DEV : (owner + 1) * CO_DEV, :]
-    copy = pltpu.make_async_copy(sums_ref, sums_hbm, sem)
-    copy.start()
-    copy.wait()
 
 
 def fine_kernel(
@@ -256,7 +253,7 @@
     vmem = pltpu.VMEM
     dma = pltpu.SemaphoreType.DMA
     square = 2 * width * width
-    blocks = shape((group, CO_DEV, width), BF16)
+    blocks = pltpu.VMEM((group, CO_DEV, width), BF16)
     ids = lambda a: a[None, :]
 
     (heads,) = call(
@@ -295,8 +292,7 @@
     from_even, from_odd = pair(to_even, 0), pair(to_odd, 1)
     new_coarse, sums = call(
         coarse_kernel, "coarse", (like(coarse_edges), blocks),
-        [lat, cedges, coarse_part, gather, picks, w_ends, w_out], out_specs=[VMEM, ANY],
-        scratch=[vmem(blocks.shape, BF16), dma(())],
+        [lat, cedges, coarse_part, gather, picks, w_ends, w_out],
     )
     got = lax.all_to_all(sums, GROUP_AXES, 0, 0, axis_index_groups=[order(group, SECOND)])
     new_edges, new_coarse, rest, agg, node_part, wn_agg, wn_out = call(

time: 26.5 us -> 26.5 us (level)
  no operation moved by 1% of the time
where the time goes in v5:
time: 26.5 us; the launch traced here: 26.1 us
  starting transfers between devices  14.8 us (56%)
  Pallas kernels  9.83 us (37%)
  waiting for transfers between devices  0.85 us (3%)
  between operations  0.67 us (3%)
    pallas_call x5, Pallas kernels, call(): pl.pallas_call(kernel, out_shape=outs, in_specs=[ANY if i in hbm else VME...  9.83 us
    all_to_all x1, starting transfers between devices, body(): lax.all_to_all(heads, GROUP_AXES, 0, 0, axis_index_groups=[order(group, F...  7.84 us
    all_to_all x1, starting transfers between devices, body(): lax.all_to_all(sums, GROUP_AXES, 0, 0, axis_index_groups=[order(group, SE...  4.37 us
    ppermute x2, starting transfers between devices, pair(): return lax.ppermute(value, GROUP_AXES, pairs + [(b, a) for a, b in pairs])  2.54 us
  transfers between devices with their start and end apart: 4, of which 2 were waited for; matrix products, arithmetic and copies ran while one was open for 0% of the time, Pallas kernels for 28%

profile of v5, /device:TPU:0, one launch (start us, length us, event | category | flops | bytes accessed | tf_op | source)
XLA Modules:
  0.0 26.1 jit_solution(2904562546082326101)
XLA Ops:
  0.6 1.4 %head.1.after = bf16[16,4,512]{2,1,0:T(4,128)(2,1)} custom-call(bf16[128,512]{1,0:T(8,128)(2,1)} %nodes_hbm.3), custom_call_target="tpu_custom_call" | custom-call | tf_op jit(solution)/shard_map/head/pallas_call | solution.py:218
  2.0 7.8 %all-to-all-start = ((bf16[16,4,512]{2,1,0:T(4,128)(2,1)}), bf16[16,4,512]{2,1,0:T(4,128)(2,1)S(1)}, u32[]{:S(2)}, u32[]{:S(2)}) async-start(bf16[16,4,512]{2,1,0:T(4,128)(2,1)} %head.1.after), calls=%async_computation | async-start | bytes 131072 | tf_op jit(solution)/shard_map/all_to_all | solution.py:262
  9.8 1.8 %load.1 = (bf16[128,512]{1,0:T(8,128)(2,1)S(1)}, bf16[64,512]{1,0:T(8,128)(2,1)S(1)}, bf16[1024,512]{1,0:T(8,128)(2,1)S(1)}, bf16[512,512]{1,0:T(8,128)(2,1)S(1)...) custom-call(bf16[128,512]{1,0:T(8,128)(2,1)} %nodes_hbm.3, ...), custom_call_target="tpu_custom_call" | custom-call | flops 268435456 | tf_op jit(solution)/shard_map/load/pallas_call | solution.py:218
  11.6 0.2 collective-permute-start
  11.8 2.3 %collective-permute-start.1 = (bf16[16,512]{1,0:T(8,128)(2,1)S(1)}, bf16[16,512]{1,0:T(8,128)(2,1)S(1)}, u32[]{:S(2)}, u32[]{:S(2)}) collective-permute-start(bf16[16,512]{1,0:T(8,128)(2,1)S(1)} %get-tuple-element.32), channel_id=1, source_target_pairs={{1,2},{3,4},{5,6},{7,8},{9,10},{11,12},{13,14},{15,0},{2,1},{4,3},... | collective-permute-start | bytes 49160 | tf_op jit(solution)/shard_map/ppermute | solution.py:26
  14.2 0.3 %all-to-all-done.lat_ref = bf16[16,4,512]{2,1,0:T(4,128)(2,1)S(1)} async-done(((bf16[16,4,512]{2,1,0:T(4,128)(2,1)}), bf16[16,4,512]{2,1,0:T(4,128)(2,1)S(1)}, u32[]{:S(2)}, u32[]{:S(2)}) %all-to-all-start) | async-done | bytes 65568 | tf_op jit(solution)/shard_map/all_to_all | solution.py:262
  14.5 1.5 %coarse.1 = (bf16[64,512]{1,0:T(8,128)(2,1)S(1)}, bf16[16,4,512]{2,1,0:T(4,128)(2,1)}) custom-call(bf16[16,4,512]{2,1,0:T(4,128)(2,1)S(1)} %all-to-all-done.lat_ref, bf16[64,512]{1,0:T(8,128)(2,1)S(1)} %get-tuple-element.23.edges_ref, f32[64,512]{1,0:T(8,128)S(1)} %get-tuple-element.24.part_ref, bf16[128,64]{1,0:T(8,128)(2,1)S(1)} %get-tuple-element.25.gather_ref, ...), custom_call_target="tpu_custom_call" | custom-call | tf_op jit(solution)/shard_map/coarse/pallas_call | solution.py:218
  16.0 4.4 %all-to-all-start.1 = ((bf16[16,4,512]{2,1,0:T(4,128)(2,1)}), bf16[16,4,512]{2,1,0:T(4,128)(2,1)S(1)}, u32[]{:S(2)}, u32[]{:S(2)}) async-start(bf16[16,4,512]{2,1,0:T(4,128)(2,1)} %get-tuple-element.29.after), calls=%async_computation.1 | async-start | bytes 131072 | tf_op jit(solution)/shard_map/all_to_all | solution.py:297
  20.4 0.0 collective-permute-done.even_ref
  20.4 0.0 collective-permute-done.1.odd_ref
  20.4 4.1 %fine.1 = (bf16[512,512]{1,0:T(8,128)(2,1)}, bf16[64,512]{1,0:T(8,128)(2,1)}, bf16[128,512]{1,0:T(8,128)(2,1)S(1)}, f32[16,512]{1,0:T(8,128)S(1)}, f32[16,512]{1...) custom-call(bf16[16,512]{1,0:T(8,128)(2,1)S(1)} %collective-permute-done.even_ref, ...), custom_call_target="tpu_custom_call" | custom-call | flops 17179869184 | tf_op jit(solution)/shard_map/fine/pallas_call | solution.py:218
  24.4 0.5 %all-to-all-done.1.got_ref = bf16[16,4,512]{2,1,0:T(4,128)(2,1)S(1)} async-done(((bf16[16,4,512]{2,1,0:T(4,128)(2,1)}), bf16[16,4,512]{2,1,0:T(4,128)(2,1)S(1)}, u32[]{:S(2)}, u32[]{:S(2)}) %all-to-all-start.1) | async-done | bytes 65568 | tf_op jit(solution)/shard_map/all_to_all | solution.py:297
  25.0 1.1 %top.1 = bf16[128,512]{1,0:T(8,128)(2,1)} custom-call(bf16[16,4,512]{2,1,0:T(4,128)(2,1)S(1)} %all-to-all-done.1.got_ref, f32[16,512]{1,0:T(8,128)S(1)} %get-tuple-element.36.agg_ref, f32[16,512]{1,0:T(8,128)S(1)} %get-tuple-element.37.part_ref, bf16[128,512]{1,0:T(8,128)(2,1)S(1)} %get-tuple-element.31.nodes_ref, ...), custom_call_target="tpu_custom_call" | custom-call | tf_op jit(solution)/shard_map/top/pallas_call | solution.py:218
Async XLA Ops:
  2.0 12.5 %all-to-all-start = ((bf16[16,4,512]{2,1,0:T(4,128)(2,1)}), bf16[16,4,512]{2,1,0:T(4,128)(2,1)S(1)}, u32[]{:S(2)}, u32[]{:S(2)}) async-start(bf16[16,4,512]{2,1,0:T(4,128)(2,1)} %head.1.after), calls=%async_computation | async-start | bytes 131072 | tf_op jit(solution)/shard_map/all_to_all | solution.py:262
  11.6 8.7 %collective-permute-start = (bf16[16,512]{1,0:T(8,128)(2,1)S(1)}, bf16[16,512]{1,0:T(8,128)(2,1)S(1)}, u32[]{:S(2)}, u32[]{:S(2)}) collective-permute-start(bf16[16,512]{1,0:T(8,128)(2,1)S(1)} %get-tuple-element.30), channel_id=1, source_target_pairs={{0,1},{2,3},{4,5},{6,7},{8,9},{10,11},{12,13},{14,15},{1,0},{3,2},... | collective-permute-start | bytes 49160 | tf_op jit(solution)/shard_map/ppermute | solution.py:26
  11.8 8.5 %collective-permute-start.1 = (bf16[16,512]{1,0:T(8,128)(2,1)S(1)}, bf16[16,512]{1,0:T(8,128)(2,1)S(1)}, u32[]{:S(2)}, u32[]{:S(2)}) collective-permute-start(bf16[16,512]{1,0:T(8,128)(2,1)S(1)} %get-tuple-element.32), channel_id=1, source_target_pairs={{1,2},{3,4},{5,6},{7,8},{9,10},{11,12},{13,14},{15,0},{2,1},{4,3},... | collective-permute-start | bytes 49160 | tf_op jit(solution)/shard_map/ppermute | solution.py:26
  16.0 9.0 %all-to-all-start.1 = ((bf16[16,4,512]{2,1,0:T(4,128)(2,1)}), bf16[16,4,512]{2,1,0:T(4,128)(2,1)S(1)}, u32[]{:S(2)}, u32[]{:S(2)}) async-start(bf16[16,4,512]{2,1,0:T(4,128)(2,1)} %get-tuple-element.29.after), calls=%async_computation.1 | async-start | bytes 131072 | tf_op jit(solution)/shard_map/all_to_all | solution.py:297

commit v6 on v5

--- a/solution.py
+++ b/solution.py
@@ -10,14 +10,14 @@
 TOP = 16
 STEP = 512
 MIB = 1 << 20
-FIRST, SECOND = 2, 2
+FIRST, SECOND = 4, 5
 ANY = pl.BlockSpec(memory_space=pl.ANY)
 VMEM = pl.BlockSpec(memory_space=pltpu.VMEM)
 BF16, F32 = jnp.bfloat16, jnp.float32
 
 
-def order(group, quarter):
-    return [(i + group * quarter // 4) % group for i in range(group)]
+def order(group, eighth):
+    return [(i + group * eighth // 8) % group for i in range(group)]
 
 
 def pair(value, first):
@@ -44,10 +44,13 @@
     return half + half * jnp.tanh(half)
 
 
-def norm_parts(values):
-    mean = jnp.mean(values, axis=-1, keepdims=True)
-    centred = values - mean
-    return centred, lax.rsqrt(jnp.mean(centred * centred, axis=-1, keepdims=True) + 1e-05)
+def centre(weights):
+    values = weights.astype(F32)
+    return (values - jnp.mean(values, axis=-1, keepdims=True)).astype(BF16)
+
+
+def spread(centred):
+    return lax.rsqrt(jnp.mean(centred * centred, axis=-1, keepdims=True) + 1e-05)
 
 
 def head_kernel(nodes_hbm, heads_ref, rows_ref, sem):
@@ -70,16 +73,16 @@
     nodes_hbm, lists_hbm, cedges_hbm, w_in_hbm, csend_hbm, crecv_hbm, w_out_hbm, send_hbm, recv_hbm, after,
     nodes_ref, cedges_ref, w_ends_ref, w_out_ref, send_ref, recv_ref,
     even_ref, odd_ref, gather_ref, picks_ref, part_ref,
-    lists_ref, w_self_ref, csend_ref, crecv_ref, sems,
+    lists_ref, w_self_ref, w_raw_ref, csend_ref, crecv_ref, sems,
 ):
     width = nodes_ref.shape[1]
     copies = start_copies(
         [
-            nodes_hbm, lists_hbm, cedges_hbm, w_in_hbm.at[pl.ds(0, width)], csend_hbm, crecv_hbm,
-            w_in_hbm.at[pl.ds(width, 2 * width)], w_out_hbm, send_hbm, recv_hbm,
+            nodes_hbm, lists_hbm, w_out_hbm, cedges_hbm, w_in_hbm.at[pl.ds(0, width)], csend_hbm, crecv_hbm,
+            w_in_hbm.at[pl.ds(width, 2 * width)], send_hbm, recv_hbm,
         ],
         [
-            nodes_ref, lists_ref, cedges_ref, w_self_ref, csend_ref, crecv_ref, w_ends_ref, w_out_ref, send_ref, recv_ref,
+            nodes_ref, lists_ref, w_raw_ref, cedges_ref, w_self_ref, csend_ref, crecv_ref, w_ends_ref, send_ref, recv_ref,
         ],
         sems,
     )
@@ -94,7 +97,9 @@
     second = lists[1:2, :] * (1 - odd) + lists[0:1, :] * odd
     even_ref[...] = dot_t(onehot_t(count, first), nodes).astype(BF16)
     odd_ref[...] = dot_t(onehot_t(count, second), nodes).astype(BF16)
-    for copy in copies[2:6]:
+    copies[2].wait()
+    w_out_ref[...] = centre(w_raw_ref[...])
+    for copy in copies[3:7]:
         copy.wait()
     part_ref[...] = dot(cedges_ref[...], w_self_ref[...])
     rows, ids = picks_ref.shape
@@ -107,7 +112,7 @@
     eye = jnp.where(across, 1.0, 0.0).astype(BF16)
     gather_ref[0:ids, :] = dot_t(send, eye).astype(BF16)
     gather_ref[ids:, :] = dot_t(recv, eye).astype(BF16)
-    for copy in copies[6:]:
+    for copy in copies[7:]:
         copy.wait()
 
 
@@ -120,8 +125,8 @@
     ends = dot(gather_ref[...], lat).astype(BF16)
     ends = jnp.concatenate([ends[0:count], ends[count:]], axis=1)
     hidden = silu(part_ref[...] + dot(ends, w_ends_ref[...])).astype(BF16)
-    centred, scale = norm_parts(dot(hidden, w_out_ref[...]))
-    new = (edges_ref[...].astype(F32) + centred * scale).astype(BF16)
+    centred = dot(hidden, w_out_ref[...])
+    new = (edges_ref[...].astype(F32) + centred * spread(centred)).astype(BF16)
     new_ref[...] = new
     sums = dot(picks_ref[...], new).astype(BF16)
     for at, owner in enumerate(order(blocks, SECOND)):
@@ -132,7 +137,7 @@
     even_ref, nodes_ref, odd_ref, w_ends_ref, w_out_ref, send_ref, recv_ref, coarse_ref,
     edges_hbm, w_in_hbm, wn_in_hbm, wn_out_hbm, after,
     new_hbm, coarse_hbm, out_ref, agg_ref, npart_ref, wn_agg_ref, wn_out_ref,
-    edges_ref, w_self_ref, wn_self_ref, new_ref, sems, out_sems,
+    edges_ref, w_self_ref, wn_self_ref, wn_raw_ref, new_ref, sems, out_sems,
 ):
     nodes = nodes_ref[...]
     count, width = nodes.shape
@@ -141,7 +146,7 @@
             edges_hbm, w_in_hbm.at[pl.ds(0, width)],
             wn_in_hbm.at[pl.ds(0, width)], wn_in_hbm.at[pl.ds(width, width)], wn_out_hbm,
         ],
-        [edges_ref, w_self_ref, wn_self_ref, wn_agg_ref, wn_out_ref],
+        [edges_ref, w_self_ref, wn_self_ref, wn_agg_ref, wn_raw_ref],
         sems,
     )
     outs = [pltpu.make_async_copy(coarse_ref, coarse_hbm, out_sems.at[0])]
@@ -166,8 +171,8 @@
         edges = edges_ref[rows, :]
         pre = pre + dot(edges, w_self_ref[...])
         hidden = silu(pre).astype(BF16)
-        centred, scale = norm_parts(dot(hidden, w_out_ref[...]))
-        new = (edges.astype(F32) + centred * (scale * valid)).astype(BF16)
+        centred = dot(hidden, w_out_ref[...])
+        new = (edges.astype(F32) + centred * (spread(centred) * valid)).astype(BF16)
         new_ref[rows, :] = new
         copy = pltpu.make_async_copy(new_ref.at[rows], new_hbm.at[rows], out_sems.at[at // STEP + 1])
         copy.start()
@@ -176,12 +181,13 @@
     agg_ref[...] = total[0:TOP]
     for copy in copies[2:]:
         copy.wait()
+    wn_out_ref[...] = centre(wn_raw_ref[...])
     pre = dot(nodes, wn_self_ref[...])
     npart_ref[...] = pre[0:TOP]
     pre = pre + dot(total.astype(BF16), wn_agg_ref[...])
     hidden = silu(pre).astype(BF16)
-    centred, scale = norm_parts(dot(hidden, wn_out_ref[...]))
-    out_ref[...] = (nodes.astype(F32) + centred * scale).astype(BF16)
+    centred = dot(hidden, wn_out_ref[...])
+    out_ref[...] = (nodes.astype(F32) + centred * spread(centred)).astype(BF16)
     for copy in outs:
         copy.wait()
 
@@ -198,8 +204,8 @@
     sums = jnp.concatenate([terms[0], jnp.zeros((TOP - CO_DEV, width), F32)], axis=0)
     agg = (agg_ref[...] + sums).astype(BF16)
     hidden = silu(part_ref[...] + dot(agg, wn_agg_ref[...])).astype(BF16)
-    centred, scale = norm_parts(dot(hidden, wn_out_ref[...]))
-    top_ref[...] = (nodes_ref[0:TOP, :].astype(F32) + centred * scale).astype(BF16)
+    centred = dot(hidden, wn_out_ref[...])
+    top_ref[...] = (nodes_ref[0:TOP, :].astype(F32) + centred * spread(centred)).astype(BF16)
     top = pltpu.make_async_copy(top_ref, out_hbm.at[pl.ds(0, TOP)], sems.at[1])
     top.start()
     rest.wait()
@@ -284,7 +290,7 @@
         + [heads],
         hbm=range(10),
         scratch=[
-            vmem(halo_lists.shape, jnp.int32), vmem((width, width), BF16),
+            vmem(halo_lists.shape, jnp.int32), vmem((width, width), BF16), vmem((width, width), BF16),
             vmem((1, cedge_count), jnp.int32), vmem((1, cedge_count), jnp.int32), dma((10,)),
         ],
         flops=edge_count * square,
@@ -314,7 +320,7 @@
         out_specs=[ANY] * 2 + [VMEM] * 5,
         scratch=[
             vmem(edge_latents.shape, BF16), vmem((width, width), BF16), vmem((width, width), BF16),
-            vmem(edge_latents.shape, BF16), dma((5,)), dma((edge_count // STEP + 1,)),
+            vmem((width, width), BF16), vmem(edge_latents.shape, BF16), dma((5,)), dma((edge_count // STEP + 1,)),
         ],
         flops=64 * edge_count * square,
     )

time: 26.5 us -> 26.4 us (level)
  starting transfers between devices: 14.8 us -> 15.5 us
  waiting for transfers between devices: 0.85 us -> 0.31 us
  Pallas kernels: 9.83 us -> 9.54 us
    all_to_all x1, starting transfers between devices: 4.37 us -> 5.11 us  [body(): lax.all_to_all(sums, GROUP_AXES, 0, 0, axis_index_groups=[order(group, SE...]
    all_to_all x1, waiting for transfers between devices: 0.53 us -> 0.01 us  [body(): lax.all_to_all(sums, GROUP_AXES, 0, 0, axis_index_groups=[order(group, SE...]
    pallas_call x5, Pallas kernels: 9.83 us -> 9.54 us  [call(): pl.pallas_call(kernel, out_shape=outs, in_specs=[ANY if i in hbm else VME...]
  transfers between devices with their start and end apart: 4 -> 4, of which waited for: 2 -> 1; matrix products, arithmetic and copies ran while one was open for 0% -> 0% of each run, Pallas kernels for 28% -> 27%
where the time goes in v6:
time: 26.4 us; the launch traced here: 26 us
  starting transfers between devices  15.5 us (59%)
  Pallas kernels  9.54 us (36%)
  between operations  0.68 us (3%)
  waiting for transfers between devices  0.31 us (1%)
    pallas_call x5, Pallas kernels, call(): pl.pallas_call(kernel, out_shape=outs, in_specs=[ANY if i in hbm else VME...  9.54 us
    all_to_all x1, starting transfers between devices, body(): lax.all_to_all(heads, GROUP_AXES, 0, 0, axis_index_groups=[order(group, F...  7.84 us
    all_to_all x1, starting transfers between devices, body(): lax.all_to_all(sums, GROUP_AXES, 0, 0, axis_index_groups=[order(group, SE...  5.11 us
    ppermute x2, starting transfers between devices, pair(): return lax.ppermute(value, GROUP_AXES, pairs + [(b, a) for a, b in pairs])  2.54 us
  transfers between devices with their start and end apart: 4, of which 1 were waited for; matrix products, arithmetic and copies ran while one was open for 0% of the time, Pallas kernels for 27%

profile of v6, /device:TPU:0, one launch (start us, length us, event | category | flops | bytes accessed | tf_op | source)
XLA Modules:
  0.0 26.0 jit_solution(4478313745313714674)
XLA Ops:
  0.6 1.4 %head.1.after = bf16[16,4,512]{2,1,0:T(4,128)(2,1)} custom-call(bf16[128,512]{1,0:T(8,128)(2,1)} %nodes_hbm.3), custom_call_target="tpu_custom_call" | custom-call | tf_op jit(solution)/shard_map/head/pallas_call | solution.py:224
  2.0 7.8 %all-to-all-start = ((bf16[16,4,512]{2,1,0:T(4,128)(2,1)}), bf16[16,4,512]{2,1,0:T(4,128)(2,1)S(1)}, u32[]{:S(2)}, u32[]{:S(2)}) async-start(bf16[16,4,512]{2,1,0:T(4,128)(2,1)} %head.1.after), calls=%async_computation | async-start | bytes 131072 | tf_op jit(solution)/shard_map/all_to_all | solution.py:268
  9.8 1.8 %load.1 = (bf16[128,512]{1,0:T(8,128)(2,1)S(1)}, bf16[64,512]{1,0:T(8,128)(2,1)S(1)}, bf16[1024,512]{1,0:T(8,128)(2,1)S(1)}, bf16[512,512]{1,0:T(8,128)(2,1)S(1)...) custom-call(bf16[128,512]{1,0:T(8,128)(2,1)} %nodes_hbm.3, ...), custom_call_target="tpu_custom_call" | custom-call | flops 268435456 | tf_op jit(solution)/shard_map/load/pallas_call | solution.py:224
  11.6 0.2 collective-permute-start
  11.8 2.3 %collective-permute-start.1 = (bf16[16,512]{1,0:T(8,128)(2,1)S(1)}, bf16[16,512]{1,0:T(8,128)(2,1)S(1)}, u32[]{:S(2)}, u32[]{:S(2)}) collective-permute-start(bf16[16,512]{1,0:T(8,128)(2,1)S(1)} %get-tuple-element.32), channel_id=1, source_target_pairs={{1,2},{3,4},{5,6},{7,8},{9,10},{11,12},{13,14},{15,0},{2,1},{4,3},... | collective-permute-start | bytes 49160 | tf_op jit(solution)/shard_map/ppermute | solution.py:26
  14.2 0.3 %all-to-all-done.lat_ref = bf16[16,4,512]{2,1,0:T(4,128)(2,1)S(1)} async-done(((bf16[16,4,512]{2,1,0:T(4,128)(2,1)}), bf16[16,4,512]{2,1,0:T(4,128)(2,1)S(1)}, u32[]{:S(2)}, u32[]{:S(2)}) %all-to-all-start) | async-done | bytes 65568 | tf_op jit(solution)/shard_map/all_to_all | solution.py:268
  14.5 1.4 %coarse.1 = (bf16[64,512]{1,0:T(8,128)(2,1)S(1)}, bf16[16,4,512]{2,1,0:T(4,128)(2,1)}) custom-call(bf16[16,4,512]{2,1,0:T(4,128)(2,1)S(1)} %all-to-all-done.lat_ref, bf16[64,512]{1,0:T(8,128)(2,1)S(1)} %get-tuple-element.23.edges_ref, f32[64,512]{1,0:T(8,128)S(1)} %get-tuple-element.24.part_ref, bf16[128,64]{1,0:T(8,128)(2,1)S(1)} %get-tuple-element.25.gather_ref, ...), custom_call_target="tpu_custom_call" | custom-call | tf_op jit(solution)/shard_map/coarse/pallas_call | solution.py:224
  15.9 5.1 %all-to-all-start.1 = ((bf16[16,4,512]{2,1,0:T(4,128)(2,1)}), bf16[16,4,512]{2,1,0:T(4,128)(2,1)S(1)}, u32[]{:S(2)}, u32[]{:S(2)}) async-start(bf16[16,4,512]{2,1,0:T(4,128)(2,1)} %get-tuple-element.29.after), calls=%async_computation.1 | async-start | bytes 131072 | tf_op jit(solution)/shard_map/all_to_all | solution.py:303
  21.0 0.0 collective-permute-done.even_ref
  21.0 0.0 collective-permute-done.1.odd_ref
  21.0 3.9 %fine.1 = (bf16[512,512]{1,0:T(8,128)(2,1)}, bf16[64,512]{1,0:T(8,128)(2,1)}, bf16[128,512]{1,0:T(8,128)(2,1)S(1)}, f32[16,512]{1,0:T(8,128)S(1)}, f32[16,512]{1...) custom-call(bf16[16,512]{1,0:T(8,128)(2,1)S(1)} %collective-permute-done.even_ref, ...), custom_call_target="tpu_custom_call" | custom-call | flops 17179869184 | tf_op jit(solution)/shard_map/fine/pallas_call | solution.py:224
  25.0 0.0 all-to-all-done.1.got_ref
  25.0 1.1 %top.1 = bf16[128,512]{1,0:T(8,128)(2,1)} custom-call(bf16[16,4,512]{2,1,0:T(4,128)(2,1)S(1)} %all-to-all-done.1.got_ref, f32[16,512]{1,0:T(8,128)S(1)} %get-tuple-element.36.agg_ref, f32[16,512]{1,0:T(8,128)S(1)} %get-tuple-element.37.part_ref, bf16[128,512]{1,0:T(8,128)(2,1)S(1)} %get-tuple-element.31.nodes_ref, ...), custom_call_target="tpu_custom_call" | custom-call | tf_op jit(solution)/shard_map/top/pallas_call | solution.py:224
Async XLA Ops:
  2.0 12.5 %all-to-all-start = ((bf16[16,4,512]{2,1,0:T(4,128)(2,1)}), bf16[16,4,512]{2,1,0:T(4,128)(2,1)S(1)}, u32[]{:S(2)}, u32[]{:S(2)}) async-start(bf16[16,4,512]{2,1,0:T(4,128)(2,1)} %head.1.after), calls=%async_computation | async-start | bytes 131072 | tf_op jit(solution)/shard_map/all_to_all | solution.py:268
  11.6 9.4 %collective-permute-start = (bf16[16,512]{1,0:T(8,128)(2,1)S(1)}, bf16[16,512]{1,0:T(8,128)(2,1)S(1)}, u32[]{:S(2)}, u32[]{:S(2)}) collective-permute-start(bf16[16,512]{1,0:T(8,128)(2,1)S(1)} %get-tuple-element.30), channel_id=1, source_target_pairs={{0,1},{2,3},{4,5},{6,7},{8,9},{10,11},{12,13},{14,15},{1,0},{3,2},... | collective-permute-start | bytes 49160 | tf_op jit(solution)/shard_map/ppermute | solution.py:26
  11.8 9.2 %collective-permute-start.1 = (bf16[16,512]{1,0:T(8,128)(2,1)S(1)}, bf16[16,512]{1,0:T(8,128)(2,1)S(1)}, u32[]{:S(2)}, u32[]{:S(2)}) collective-permute-start(bf16[16,512]{1,0:T(8,128)(2,1)S(1)} %get-tuple-element.32), channel_id=1, source_target_pairs={{1,2},{3,4},{5,6},{7,8},{9,10},{11,12},{13,14},{15,0},{2,1},{4,3},... | collective-permute-start | bytes 49160 | tf_op jit(solution)/shard_map/ppermute | solution.py:26
  15.9 9.0 %all-to-all-start.1 = ((bf16[16,4,512]{2,1,0:T(4,128)(2,1)}), bf16[16,4,512]{2,1,0:T(4,128)(2,1)S(1)}, u32[]{:S(2)}, u32[]{:S(2)}) async-start(bf16[16,4,512]{2,1,0:T(4,128)(2,1)} %get-tuple-element.29.after), calls=%async_computation.1 | async-start | bytes 131072 | tf_op jit(solution)/shard_map/all_to_all | solution.py:303

commit v7 on v5

--- a/solution.py
+++ b/solution.py
@@ -136,14 +136,7 @@
 ):
     nodes = nodes_ref[...]
     count, width = nodes.shape
-    copies = start_copies(
-        [
-            edges_hbm, w_in_hbm.at[pl.ds(0, width)],
-            wn_in_hbm.at[pl.ds(0, width)], wn_in_hbm.at[pl.ds(width, width)], wn_out_hbm,
-        ],
-        [edges_ref, w_self_ref, wn_self_ref, wn_agg_ref, wn_out_ref],
-        sems,
-    )
+    copies = start_copies([edges_hbm, w_in_hbm.at[pl.ds(0, width)]], [edges_ref, w_self_ref], sems.at[0])
     outs = [pltpu.make_async_copy(coarse_ref, coarse_hbm, out_sems.at[0])]
     outs[0].start()
     odd = (lax.axis_index(GROUP_AXES) % 2).astype(F32)
@@ -161,8 +154,13 @@
         valid = dot_t(picks, ones)[:, 0:1]
         pre = dot(jnp.concatenate([senders, receivers], axis=1), w_ends_ref[...])
         if at == 0:
-            for copy in copies[:2]:
+            for copy in copies:
                 copy.wait()
+            copies = start_copies(
+                [wn_in_hbm.at[pl.ds(0, width)], wn_in_hbm.at[pl.ds(width, width)], wn_out_hbm],
+                [wn_self_ref, wn_agg_ref, wn_out_ref],
+                sems.at[1],
+            )
         edges = edges_ref[rows, :]
         pre = pre + dot(edges, w_self_ref[...])
         hidden = silu(pre).astype(BF16)
@@ -174,7 +172,7 @@
         outs.append(copy)
         total = total + dot(picks, new)
     agg_ref[...] = total[0:TOP]
-    for copy in copies[2:]:
+    for copy in copies:
         copy.wait()
     pre = dot(nodes, wn_self_ref[...])
     npart_ref[...] = pre[0:TOP]
@@ -314,7 +312,7 @@
         out_specs=[ANY] * 2 + [VMEM] * 5,
         scratch=[
             vmem(edge_latents.shape, BF16), vmem((width, width), BF16), vmem((width, width), BF16),
-            vmem(edge_latents.shape, BF16), dma((5,)), dma((edge_count // STEP + 1,)),
+            vmem(edge_latents.shape, BF16), dma((2, 3)), dma((edge_count // STEP + 1,)),
         ],
         flops=64 * edge_count * square,
     )

time: 26.5 us -> 26.5 us (level)
  Pallas kernels: 9.83 us -> 10.2 us
  waiting for transfers between devices: 0.85 us -> 0.5 us
    pallas_call x5, Pallas kernels: 9.83 us -> 10.2 us  [call(): pl.pallas_call(kernel, out_shape=outs, in_specs=[ANY if i in hbm else VME...]
    all_to_all x1, waiting for transfers between devices: 0.53 us -> 0.17 us  [body(): lax.all_to_all(sums, GROUP_AXES, 0, 0, axis_index_groups=[order(group, SE...]
  transfers between devices with their start and end apart: 4 -> 4, of which waited for: 2 -> 2; matrix products, arithmetic and copies ran while one was open for 0% -> 0% of each run, Pallas kernels for 28% -> 29%
where the time goes in v7:
time: 26.5 us; the launch traced here: 26.1 us
  starting transfers between devices  14.8 us (56%)
  Pallas kernels  10.2 us (38%)
  between operations  0.67 us (3%)
  waiting for transfers between devices  0.5 us (2%)
    pallas_call x5, Pallas kernels, call(): pl.pallas_call(kernel, out_shape=outs, in_specs=[ANY if i in hbm else VME...  10.2 us
    all_to_all x1, starting transfers between devices, body(): lax.all_to_all(heads, GROUP_AXES, 0, 0, axis_index_groups=[order(group, F...  7.84 us
    all_to_all x1, starting transfers between devices, body(): lax.all_to_all(sums, GROUP_AXES, 0, 0, axis_index_groups=[order(group, SE...  4.37 us
    ppermute x2, starting transfers between devices, pair(): return lax.ppermute(value, GROUP_AXES, pairs + [(b, a) for a, b in pairs])  2.54 us
  transfers between devices with their start and end apart: 4, of which 2 were waited for; matrix products, arithmetic and copies ran while one was open for 0% of the time, Pallas kernels for 29%

profile of v7, /device:TPU:0, one launch (start us, length us, event | category | flops | bytes accessed | tf_op | source)
XLA Modules:
  0.0 26.1 jit_solution(10776210126992012912)
XLA Ops:
  0.6 1.4 %head.1.after = bf16[16,4,512]{2,1,0:T(4,128)(2,1)} custom-call(bf16[128,512]{1,0:T(8,128)(2,1)} %nodes_hbm.3), custom_call_target="tpu_custom_call" | custom-call | tf_op jit(solution)/shard_map/head/pallas_call | solution.py:216
  2.0 7.8 %all-to-all-start = ((bf16[16,4,512]{2,1,0:T(4,128)(2,1)}), bf16[16,4,512]{2,1,0:T(4,128)(2,1)S(1)}, u32[]{:S(2)}, u32[]{:S(2)}) async-start(bf16[16,4,512]{2,1,0:T(4,128)(2,1)} %head.1.after), calls=%async_computation | async-start | bytes 131072 | tf_op jit(solution)/shard_map/all_to_all | solution.py:260
  9.8 1.8 %load.1 = (bf16[128,512]{1,0:T(8,128)(2,1)S(1)}, bf16[64,512]{1,0:T(8,128)(2,1)S(1)}, bf16[1024,512]{1,0:T(8,128)(2,1)S(1)}, bf16[512,512]{1,0:T(8,128)(2,1)S(1)...) custom-call(bf16[128,512]{1,0:T(8,128)(2,1)} %nodes_hbm.3, ...), custom_call_target="tpu_custom_call" | custom-call | flops 268435456 | tf_op jit(solution)/shard_map/load/pallas_call | solution.py:216
  11.6 0.2 collective-permute-start
  11.8 2.3 %collective-permute-start.1 = (bf16[16,512]{1,0:T(8,128)(2,1)S(1)}, bf16[16,512]{1,0:T(8,128)(2,1)S(1)}, u32[]{:S(2)}, u32[]{:S(2)}) collective-permute-start(bf16[16,512]{1,0:T(8,128)(2,1)S(1)} %get-tuple-element.32), channel_id=1, source_target_pairs={{1,2},{3,4},{5,6},{7,8},{9,10},{11,12},{13,14},{15,0},{2,1},{4,3},... | collective-permute-start | bytes 49160 | tf_op jit(solution)/shard_map/ppermute | solution.py:26
  14.2 0.3 %all-to-all-done.lat_ref = bf16[16,4,512]{2,1,0:T(4,128)(2,1)S(1)} async-done(((bf16[16,4,512]{2,1,0:T(4,128)(2,1)}), bf16[16,4,512]{2,1,0:T(4,128)(2,1)S(1)}, u32[]{:S(2)}, u32[]{:S(2)}) %all-to-all-start) | async-done | bytes 65568 | tf_op jit(solution)/shard_map/all_to_all | solution.py:260
  14.5 1.5 %coarse.1 = (bf16[64,512]{1,0:T(8,128)(2,1)S(1)}, bf16[16,4,512]{2,1,0:T(4,128)(2,1)}) custom-call(bf16[16,4,512]{2,1,0:T(4,128)(2,1)S(1)} %all-to-all-done.lat_ref, bf16[64,512]{1,0:T(8,128)(2,1)S(1)} %get-tuple-element.23.edges_ref, f32[64,512]{1,0:T(8,128)S(1)} %get-tuple-element.24.part_ref, bf16[128,64]{1,0:T(8,128)(2,1)S(1)} %get-tuple-element.25.gather_ref, ...), custom_call_target="tpu_custom_call" | custom-call | tf_op jit(solution)/shard_map/coarse/pallas_call | solution.py:216
  16.0 4.4 %all-to-all-start.1 = ((bf16[16,4,512]{2,1,0:T(4,128)(2,1)}), bf16[16,4,512]{2,1,0:T(4,128)(2,1)S(1)}, u32[]{:S(2)}, u32[]{:S(2)}) async-start(bf16[16,4,512]{2,1,0:T(4,128)(2,1)} %get-tuple-element.29.after), calls=%async_computation.1 | async-start | bytes 131072 | tf_op jit(solution)/shard_map/all_to_all | solution.py:295
  20.4 0.0 collective-permute-done.even_ref
  20.4 0.0 collective-permute-done.1.odd_ref
  20.4 4.4 %fine.1 = (bf16[512,512]{1,0:T(8,128)(2,1)}, bf16[64,512]{1,0:T(8,128)(2,1)}, bf16[128,512]{1,0:T(8,128)(2,1)S(1)}, f32[16,512]{1,0:T(8,128)S(1)}, f32[16,512]{1...) custom-call(bf16[16,512]{1,0:T(8,128)(2,1)S(1)} %collective-permute-done.even_ref, ...), custom_call_target="tpu_custom_call" | custom-call | flops 17179869184 | tf_op jit(solution)/shard_map/fine/pallas_call | solution.py:216
  24.8 0.2 all-to-all-done.1.got_ref
  25.0 1.1 %top.1 = bf16[128,512]{1,0:T(8,128)(2,1)} custom-call(bf16[16,4,512]{2,1,0:T(4,128)(2,1)S(1)} %all-to-all-done.1.got_ref, f32[16,512]{1,0:T(8,128)S(1)} %get-tuple-element.36.agg_ref, f32[16,512]{1,0:T(8,128)S(1)} %get-tuple-element.37.part_ref, bf16[128,512]{1,0:T(8,128)(2,1)S(1)} %get-tuple-element.31.nodes_ref, ...), custom_call_target="tpu_custom_call" | custom-call | tf_op jit(solution)/shard_map/top/pallas_call | solution.py:216
Async XLA Ops:
  2.0 12.5 %all-to-all-start = ((bf16[16,4,512]{2,1,0:T(4,128)(2,1)}), bf16[16,4,512]{2,1,0:T(4,128)(2,1)S(1)}, u32[]{:S(2)}, u32[]{:S(2)}) async-start(bf16[16,4,512]{2,1,0:T(4,128)(2,1)} %head.1.after), calls=%async_computation | async-start | bytes 131072 | tf_op jit(solution)/shard_map/all_to_all | solution.py:260
  11.6 8.7 %collective-permute-start = (bf16[16,512]{1,0:T(8,128)(2,1)S(1)}, bf16[16,512]{1,0:T(8,128)(2,1)S(1)}, u32[]{:S(2)}, u32[]{:S(2)}) collective-permute-start(bf16[16,512]{1,0:T(8,128)(2,1)S(1)} %get-tuple-element.30), channel_id=1, source_target_pairs={{0,1},{2,3},{4,5},{6,7},{8,9},{10,11},{12,13},{14,15},{1,0},{3,2},... | collective-permute-start | bytes 49160 | tf_op jit(solution)/shard_map/ppermute | solution.py:26
  11.8 8.5 %collective-permute-start.1 = (bf16[16,512]{1,0:T(8,128)(2,1)S(1)}, bf16[16,512]{1,0:T(8,128)(2,1)S(1)}, u32[]{:S(2)}, u32[]{:S(2)}) collective-permute-start(bf16[16,512]{1,0:T(8,128)(2,1)S(1)} %get-tuple-element.32), channel_id=1, source_target_pairs={{1,2},{3,4},{5,6},{7,8},{9,10},{11,12},{13,14},{15,0},{2,1},{4,3},... | collective-permute-start | bytes 49160 | tf_op jit(solution)/shard_map/ppermute | solution.py:26
  16.0 9.0 %all-to-all-start.1 = ((bf16[16,4,512]{2,1,0:T(4,128)(2,1)}), bf16[16,4,512]{2,1,0:T(4,128)(2,1)S(1)}, u32[]{:S(2)}, u32[]{:S(2)}) async-start(bf16[16,4,512]{2,1,0:T(4,128)(2,1)} %get-tuple-element.29.after), calls=%async_computation.1 | async-start | bytes 131072 | tf_op jit(solution)/shard_map/all_to_all | solution.py:295

commit v8 on v5

--- a/solution.py
+++ b/solution.py
@@ -10,14 +10,14 @@
 TOP = 16
 STEP = 512
 MIB = 1 << 20
-FIRST, SECOND = 2, 2
 ANY = pl.BlockSpec(memory_space=pl.ANY)
 VMEM = pl.BlockSpec(memory_space=pltpu.VMEM)
 BF16, F32 = jnp.bfloat16, jnp.float32
 
 
-def order(group, quarter):
-    return [(i + group * quarter // 4) % group for i in range(group)]
+def order(group, sub):
+    patch = group // sub
+    return [(i + patch // 2) % patch * sub + j for j in range(sub) for i in range(patch)]
 
 
 def pair(value, first):
@@ -99,7 +99,10 @@
     part_ref[...] = dot(cedges_ref[...], w_self_ref[...])
     rows, ids = picks_ref.shape
     at = lax.broadcasted_iota(jnp.int32, (rows, ids), 0)
-    node = (at + CO_DEV * order(rows // CO_DEV, FIRST)[0]) % rows
+    sub, patch = lax.axis_size("sub"), lax.axis_size("patch")
+    block = at // CO_DEV
+    device = (block % patch + patch // 2) % patch * sub + block // patch
+    node = device * CO_DEV + at % CO_DEV
     send = jnp.where(node == csend_ref[...], 1.0, 0.0).astype(BF16)
     recv = jnp.where(node == crecv_ref[...], 1.0, 0.0).astype(BF16)
     picks_ref[...] = onehot_t(rows, crecv_ref[...])
@@ -124,7 +127,7 @@
     new = (edges_ref[...].astype(F32) + centred * scale).astype(BF16)
     new_ref[...] = new
     sums = dot(picks_ref[...], new).astype(BF16)
-    for at, owner in enumerate(order(blocks, SECOND)):
+    for at, owner in enumerate(order(blocks, lax.axis_size("sub"))):
         sums_ref[at] = sums[owner * CO_DEV : (owner + 1) * CO_DEV, :]
 
 
@@ -248,6 +251,7 @@
     halo = halo_lists.shape[2]
     group = lax.axis_size(GROUP_AXES)
     coarse_count = group * CO_DEV
+    sub = lax.axis_size("sub")
     shape = jax.ShapeDtypeStruct
     like = lambda a: shape(a.shape, a.dtype)
     vmem = pltpu.VMEM
@@ -259,7 +263,7 @@
     (heads,) = call(
         head_kernel, "head", (blocks,), in_hbm(node_latents), hbm=(0,), scratch=[vmem((TOP, width), BF16), dma(())],
     )
-    lat = lax.all_to_all(heads, GROUP_AXES, 0, 0, axis_index_groups=[order(group, FIRST)])
+    lat = lax.all_to_all(heads, GROUP_AXES, 0, 0, axis_index_groups=[order(group, sub)])
     send, recv = ids(fine_senders), ids(fine_receivers)
     nodes, cedges, w_ends, w_out, send, recv, to_even, to_odd, gather, picks, coarse_part = call(
         load_kernel,
@@ -294,7 +298,7 @@
         coarse_kernel, "coarse", (like(coarse_edges), blocks),
         [lat, cedges, coarse_part, gather, picks, w_ends, w_out],
     )
-    got = lax.all_to_all(sums, GROUP_AXES, 0, 0, axis_index_groups=[order(group, SECOND)])
+    got = lax.all_to_all(sums, GROUP_AXES, 0, 0, axis_index_groups=[order(group, sub)])
     new_edges, new_coarse, rest, agg, node_part, wn_agg, wn_out = call(
         fine_kernel,
         "fine",

time: 26.5 us -> 26.3 us (level)
  waiting for transfers between devices: 0.85 us -> 0.56 us
    all_to_all x2, waiting for transfers between devices: 0.85 us -> 0.56 us  [the longest x1 0.41 us: body(): lax.all_to_all(sums, GROUP_AXES, 0, 0, axis_index_groups=[order(group, su...]
where the time goes in v8:
time: 26.3 us; the launch traced here: 25.9 us
  starting transfers between devices  14.8 us (56%)
  Pallas kernels  9.84 us (37%)
  between operations  0.67 us (3%)
  waiting for transfers between devices  0.56 us (2%)
    pallas_call x5, Pallas kernels, call(): pl.pallas_call(kernel, out_shape=outs, in_specs=[ANY if i in hbm else VME...  9.84 us
    all_to_all x1, starting transfers between devices, body(): lax.all_to_all(heads, GROUP_AXES, 0, 0, axis_index_groups=[order(group, s...  7.84 us
    all_to_all x1, starting transfers between devices, body(): lax.all_to_all(sums, GROUP_AXES, 0, 0, axis_index_groups=[order(group, su...  4.45 us
    ppermute x2, starting transfers between devices, pair(): return lax.ppermute(value, GROUP_AXES, pairs + [(b, a) for a, b in pairs])  2.54 us
  transfers between devices with their start and end apart: 4, of which 2 were waited for; matrix products, arithmetic and copies ran while one was open for 0% of the time, Pallas kernels for 28%

profile of v8, /device:TPU:0, one launch (start us, length us, event | category | flops | bytes accessed | tf_op | source)
XLA Modules:
  0.0 25.9 jit_solution(8978223142487173694)
XLA Ops:
  0.6 1.4 %head.1.after = bf16[16,4,512]{2,1,0:T(4,128)(2,1)} custom-call(bf16[128,512]{1,0:T(8,128)(2,1)} %nodes_hbm.3), custom_call_target="tpu_custom_call" | custom-call | tf_op jit(solution)/shard_map/head/pallas_call | solution.py:221
  2.0 7.8 %all-to-all-start = ((bf16[16,4,512]{2,1,0:T(4,128)(2,1)}), bf16[16,4,512]{2,1,0:T(4,128)(2,1)S(1)}, u32[]{:S(2)}, u32[]{:S(2)}) async-start(bf16[16,4,512]{2,1,0:T(4,128)(2,1)} %head.1.after), calls=%async_computation | async-start | bytes 131072 | tf_op jit(solution)/shard_map/all_to_all | solution.py:266
  9.8 1.8 %load.1 = (bf16[128,512]{1,0:T(8,128)(2,1)S(1)}, bf16[64,512]{1,0:T(8,128)(2,1)S(1)}, bf16[1024,512]{1,0:T(8,128)(2,1)S(1)}, bf16[512,512]{1,0:T(8,128)(2,1)S(1)...) custom-call(bf16[128,512]{1,0:T(8,128)(2,1)} %nodes_hbm.3, ...), custom_call_target="tpu_custom_call" | custom-call | flops 268435456 | tf_op jit(solution)/shard_map/load/pallas_call | solution.py:221
  11.6 0.2 collective-permute-start
  11.8 2.3 %collective-permute-start.1 = (bf16[16,512]{1,0:T(8,128)(2,1)S(1)}, bf16[16,512]{1,0:T(8,128)(2,1)S(1)}, u32[]{:S(2)}, u32[]{:S(2)}) collective-permute-start(bf16[16,512]{1,0:T(8,128)(2,1)S(1)} %get-tuple-element.32), channel_id=1, source_target_pairs={{1,2},{3,4},{5,6},{7,8},{9,10},{11,12},{13,14},{15,0},{2,1},{4,3},... | collective-permute-start | bytes 49160 | tf_op jit(solution)/shard_map/ppermute | solution.py:26
  14.2 0.1 all-to-all-done.lat_ref
  14.3 1.5 %coarse.1 = (bf16[64,512]{1,0:T(8,128)(2,1)S(1)}, bf16[16,4,512]{2,1,0:T(4,128)(2,1)}) custom-call(bf16[16,4,512]{2,1,0:T(4,128)(2,1)S(1)} %all-to-all-done.lat_ref, bf16[64,512]{1,0:T(8,128)(2,1)S(1)} %get-tuple-element.23.edges_ref, f32[64,512]{1,0:T(8,128)S(1)} %get-tuple-element.24.part_ref, bf16[128,64]{1,0:T(8,128)(2,1)S(1)} %get-tuple-element.25.gather_ref, ...), custom_call_target="tpu_custom_call" | custom-call | tf_op jit(solution)/shard_map/coarse/pallas_call | solution.py:221
  15.8 4.4 %all-to-all-start.1 = ((bf16[16,4,512]{2,1,0:T(4,128)(2,1)}), bf16[16,4,512]{2,1,0:T(4,128)(2,1)S(1)}, u32[]{:S(2)}, u32[]{:S(2)}) async-start(bf16[16,4,512]{2,1,0:T(4,128)(2,1)} %get-tuple-element.29.after), calls=%async_computation.1 | async-start | bytes 131072 | tf_op jit(solution)/shard_map/all_to_all | solution.py:301
  20.3 0.0 collective-permute-done.even_ref
  20.3 0.0 collective-permute-done.1.odd_ref
  20.3 4.1 %fine.1 = (bf16[512,512]{1,0:T(8,128)(2,1)}, bf16[64,512]{1,0:T(8,128)(2,1)}, bf16[128,512]{1,0:T(8,128)(2,1)S(1)}, f32[16,512]{1,0:T(8,128)S(1)}, f32[16,512]{1...) custom-call(bf16[16,512]{1,0:T(8,128)(2,1)S(1)} %collective-permute-done.even_ref, ...), custom_call_target="tpu_custom_call" | custom-call | flops 17179869184 | tf_op jit(solution)/shard_map/fine/pallas_call | solution.py:221
  24.4 0.4 %all-to-all-done.1.got_ref = bf16[16,4,512]{2,1,0:T(4,128)(2,1)S(1)} async-done(((bf16[16,4,512]{2,1,0:T(4,128)(2,1)}), bf16[16,4,512]{2,1,0:T(4,128)(2,1)S(1)}, u32[]{:S(2)}, u32[]{:S(2)}) %all-to-all-start.1) | async-done | bytes 65568 | tf_op jit(solution)/shard_map/all_to_all | solution.py:301
  24.8 1.1 %top.1 = bf16[128,512]{1,0:T(8,128)(2,1)} custom-call(bf16[16,4,512]{2,1,0:T(4,128)(2,1)S(1)} %all-to-all-done.1.got_ref, f32[16,512]{1,0:T(8,128)S(1)} %get-tuple-element.36.agg_ref, f32[16,512]{1,0:T(8,128)S(1)} %get-tuple-element.37.part_ref, bf16[128,512]{1,0:T(8,128)(2,1)S(1)} %get-tuple-element.31.nodes_ref, ...), custom_call_target="tpu_custom_call" | custom-call | tf_op jit(solution)/shard_map/top/pallas_call | solution.py:221
Async XLA Ops:
  2.0 12.3 %all-to-all-start = ((bf16[16,4,512]{2,1,0:T(4,128)(2,1)}), bf16[16,4,512]{2,1,0:T(4,128)(2,1)S(1)}, u32[]{:S(2)}, u32[]{:S(2)}) async-start(bf16[16,4,512]{2,1,0:T(4,128)(2,1)} %head.1.after), calls=%async_computation | async-start | bytes 131072 | tf_op jit(solution)/shard_map/all_to_all | solution.py:266
  11.6 8.7 %collective-permute-start = (bf16[16,512]{1,0:T(8,128)(2,1)S(1)}, bf16[16,512]{1,0:T(8,128)(2,1)S(1)}, u32[]{:S(2)}, u32[]{:S(2)}) collective-permute-start(bf16[16,512]{1,0:T(8,128)(2,1)S(1)} %get-tuple-element.30), channel_id=1, source_target_pairs={{0,1},{2,3},{4,5},{6,7},{8,9},{10,11},{12,13},{14,15},{1,0},{3,2},... | collective-permute-start | bytes 49160 | tf_op jit(solution)/shard_map/ppermute | solution.py:26
  11.8 8.5 %collective-permute-start.1 = (bf16[16,512]{1,0:T(8,128)(2,1)S(1)}, bf16[16,512]{1,0:T(8,128)(2,1)S(1)}, u32[]{:S(2)}, u32[]{:S(2)}) collective-permute-start(bf16[16,512]{1,0:T(8,128)(2,1)S(1)} %get-tuple-element.32), channel_id=1, source_target_pairs={{1,2},{3,4},{5,6},{7,8},{9,10},{11,12},{13,14},{15,0},{2,1},{4,3},... | collective-permute-start | bytes 49160 | tf_op jit(solution)/shard_map/ppermute | solution.py:26
  15.8 9.0 %all-to-all-start.1 = ((bf16[16,4,512]{2,1,0:T(4,128)(2,1)}), bf16[16,4,512]{2,1,0:T(4,128)(2,1)S(1)}, u32[]{:S(2)}, u32[]{:S(2)}) async-start(bf16[16,4,512]{2,1,0:T(4,128)(2,1)} %get-tuple-element.29.after), calls=%async_computation.1 | async-start | bytes 131072 | tf_op jit(solution)/shard_map/all_to_all | solution.py:301

commit v9 on v8

--- a/solution.py
+++ b/solution.py
@@ -8,7 +8,6 @@
 CO_DEV = 4
 GROUP_AXES = ("patch", "sub")
 TOP = 16
-STEP = 512
 MIB = 1 << 20
 ANY = pl.BlockSpec(memory_space=pl.ANY)
 VMEM = pl.BlockSpec(memory_space=pltpu.VMEM)
@@ -154,28 +153,22 @@
     prev = (met * odd + other * (1.0 - odd)).astype(BF16)
     following = (other * odd + met * (1.0 - odd)).astype(BF16)
     extended = jnp.concatenate([prev, nodes, following], axis=0)
-    ones = jnp.ones((count, 128), BF16)
-    total = jnp.zeros((count, width), F32)
-    for at in range(0, edges_ref.shape[0], STEP):
-        rows = pl.ds(at, STEP)
-        picks = onehot_t(count, recv_ref[:, rows])
-        senders = dot_t(onehot_t(extended.shape[0], send_ref[:, rows]), extended).astype(BF16)
-        receivers = dot_t(picks, nodes).astype(BF16)
-        valid = dot_t(picks, ones)[:, 0:1]
-        pre = dot(jnp.concatenate([senders, receivers], axis=1), w_ends_ref[...])
-        if at == 0:
-            for copy in copies[:2]:
-                copy.wait()
-        edges = edges_ref[rows, :]
-        pre = pre + dot(edges, w_self_ref[...])
-        hidden = silu(pre).astype(BF16)
-        centred, scale = norm_parts(dot(hidden, w_out_ref[...]))
-        new = (edges.astype(F32) + centred * (scale * valid)).astype(BF16)
-        new_ref[rows, :] = new
-        copy = pltpu.make_async_copy(new_ref.at[rows], new_hbm.at[rows], out_sems.at[at // STEP + 1])
-        copy.start()
-        outs.append(copy)
-        total = total + dot(picks, new)
+    picks = onehot_t(count, recv_ref[...])
+    senders = dot_t(onehot_t(extended.shape[0], send_ref[...]), extended).astype(BF16)
+    receivers = dot_t(picks, nodes).astype(BF16)
+    valid = dot_t(picks, jnp.ones((count, 128), BF16))[:, 0:1]
+    pre = dot(jnp.concatenate([senders, receivers], axis=1), w_ends_ref[...])
+    for copy in copies[:2]:
+        copy.wait()
+    edges = edges_ref[...]
+    pre = pre + dot(edges, w_self_ref[...])
+    hidden = silu(pre).astype(BF16)
+    centred, scale = norm_parts(dot(hidden, w_out_ref[...]))
+    new = (edges.astype(F32) + centred * (scale * valid)).astype(BF16)
+    new_ref[...] = new
+    outs.append(pltpu.make_async_copy(new_ref, new_hbm, out_sems.at[1]))
+    outs[1].start()
+    total = dot(picks, new)
     agg_ref[...] = total[0:TOP]
     for copy in copies[2:]:
         copy.wait()
@@ -318,7 +311,7 @@
         out_specs=[ANY] * 2 + [VMEM] * 5,
         scratch=[
             vmem(edge_latents.shape, BF16), vmem((width, width), BF16), vmem((width, width), BF16),
-            vmem(edge_latents.shape, BF16), dma((5,)), dma((edge_count // STEP + 1,)),
+            vmem(edge_latents.shape, BF16), dma((5,)), dma((2,)),
         ],
         flops=64 * edge_count * square,
     )

time: 26.3 us -> 26.3 us (level)
  no operation moved by 1% of the time
where the time goes in v9:
time: 26.3 us; the launch traced here: 25.9 us
  starting transfers between devices  14.8 us (56%)
  Pallas kernels  9.84 us (37%)
  between operations  0.67 us (3%)
  waiting for transfers between devices  0.56 us (2%)
    pallas_call x5, Pallas kernels, call(): pl.pallas_call(kernel, out_shape=outs, in_specs=[ANY if i in hbm else VME...  9.84 us
    all_to_all x1, starting transfers between devices, body(): lax.all_to_all(heads, GROUP_AXES, 0, 0, axis_index_groups=[order(group, s...  7.84 us
    all_to_all x1, starting transfers between devices, body(): lax.all_to_all(sums, GROUP_AXES, 0, 0, axis_index_groups=[order(group, su...  4.45 us
    ppermute x2, starting transfers between devices, pair(): return lax.ppermute(value, GROUP_AXES, pairs + [(b, a) for a, b in pairs])  2.54 us
  transfers between devices with their start and end apart: 4, of which 2 were waited for; matrix products, arithmetic and copies ran while one was open for 0% of the time, Pallas kernels for 28%

profile of v9, /device:TPU:0, one launch (start us, length us, event | category | flops | bytes accessed | tf_op | source)
XLA Modules:
  0.0 25.9 jit_solution(8978223142487173694)
XLA Ops:
  0.6 1.4 %head.1.after = bf16[16,4,512]{2,1,0:T(4,128)(2,1)} custom-call(bf16[128,512]{1,0:T(8,128)(2,1)} %nodes_hbm.3), custom_call_target="tpu_custom_call" | custom-call | tf_op jit(solution)/shard_map/head/pallas_call | solution.py:214
  2.0 7.8 %all-to-all-start = ((bf16[16,4,512]{2,1,0:T(4,128)(2,1)}), bf16[16,4,512]{2,1,0:T(4,128)(2,1)S(1)}, u32[]{:S(2)}, u32[]{:S(2)}) async-start(bf16[16,4,512]{2,1,0:T(4,128)(2,1)} %head.1.after), calls=%async_computation | async-start | bytes 131072 | tf_op jit(solution)/shard_map/all_to_all | solution.py:259
  9.8 1.8 %load.1 = (bf16[128,512]{1,0:T(8,128)(2,1)S(1)}, bf16[64,512]{1,0:T(8,128)(2,1)S(1)}, bf16[1024,512]{1,0:T(8,128)(2,1)S(1)}, bf16[512,512]{1,0:T(8,128)(2,1)S(1)...) custom-call(bf16[128,512]{1,0:T(8,128)(2,1)} %nodes_hbm.3, ...), custom_call_target="tpu_custom_call" | custom-call | flops 268435456 | tf_op jit(solution)/shard_map/load/pallas_call | solution.py:214
  11.6 0.2 collective-permute-start
  11.8 2.3 %collective-permute-start.1 = (bf16[16,512]{1,0:T(8,128)(2,1)S(1)}, bf16[16,512]{1,0:T(8,128)(2,1)S(1)}, u32[]{:S(2)}, u32[]{:S(2)}) collective-permute-start(bf16[16,512]{1,0:T(8,128)(2,1)S(1)} %get-tuple-element.32), channel_id=1, source_target_pairs={{1,2},{3,4},{5,6},{7,8},{9,10},{11,12},{13,14},{15,0},{2,1},{4,3},... | collective-permute-start | bytes 49160 | tf_op jit(solution)/shard_map/ppermute | solution.py:25
  14.2 0.1 all-to-all-done.lat_ref
  14.3 1.5 %coarse.1 = (bf16[64,512]{1,0:T(8,128)(2,1)S(1)}, bf16[16,4,512]{2,1,0:T(4,128)(2,1)}) custom-call(bf16[16,4,512]{2,1,0:T(4,128)(2,1)S(1)} %all-to-all-done.lat_ref, bf16[64,512]{1,0:T(8,128)(2,1)S(1)} %get-tuple-element.23.edges_ref, f32[64,512]{1,0:T(8,128)S(1)} %get-tuple-element.24.part_ref, bf16[128,64]{1,0:T(8,128)(2,1)S(1)} %get-tuple-element.25.gather_ref, ...), custom_call_target="tpu_custom_call" | custom-call | tf_op jit(solution)/shard_map/coarse/pallas_call | solution.py:214
  15.8 4.4 %all-to-all-start.1 = ((bf16[16,4,512]{2,1,0:T(4,128)(2,1)}), bf16[16,4,512]{2,1,0:T(4,128)(2,1)S(1)}, u32[]{:S(2)}, u32[]{:S(2)}) async-start(bf16[16,4,512]{2,1,0:T(4,128)(2,1)} %get-tuple-element.29.after), calls=%async_computation.1 | async-start | bytes 131072 | tf_op jit(solution)/shard_map/all_to_all | solution.py:294
  20.3 0.0 collective-permute-done.even_ref
  20.3 0.0 collective-permute-done.1.odd_ref
  20.3 4.1 %fine.1 = (bf16[512,512]{1,0:T(8,128)(2,1)}, bf16[64,512]{1,0:T(8,128)(2,1)}, bf16[128,512]{1,0:T(8,128)(2,1)S(1)}, f32[16,512]{1,0:T(8,128)S(1)}, f32[16,512]{1...) custom-call(bf16[16,512]{1,0:T(8,128)(2,1)S(1)} %collective-permute-done.even_ref, ...), custom_call_target="tpu_custom_call" | custom-call | flops 17179869184 | tf_op jit(solution)/shard_map/fine/pallas_call | solution.py:214
  24.4 0.4 %all-to-all-done.1.got_ref = bf16[16,4,512]{2,1,0:T(4,128)(2,1)S(1)} async-done(((bf16[16,4,512]{2,1,0:T(4,128)(2,1)}), bf16[16,4,512]{2,1,0:T(4,128)(2,1)S(1)}, u32[]{:S(2)}, u32[]{:S(2)}) %all-to-all-start.1) | async-done | bytes 65568 | tf_op jit(solution)/shard_map/all_to_all | solution.py:294
  24.8 1.1 %top.1 = bf16[128,512]{1,0:T(8,128)(2,1)} custom-call(bf16[16,4,512]{2,1,0:T(4,128)(2,1)S(1)} %all-to-all-done.1.got_ref, f32[16,512]{1,0:T(8,128)S(1)} %get-tuple-element.36.agg_ref, f32[16,512]{1,0:T(8,128)S(1)} %get-tuple-element.37.part_ref, bf16[128,512]{1,0:T(8,128)(2,1)S(1)} %get-tuple-element.31.nodes_ref, ...), custom_call_target="tpu_custom_call" | custom-call | tf_op jit(solution)/shard_map/top/pallas_call | solution.py:214
Async XLA Ops:
  2.0 12.3 %all-to-all-start = ((bf16[16,4,512]{2,1,0:T(4,128)(2,1)}), bf16[16,4,512]{2,1,0:T(4,128)(2,1)S(1)}, u32[]{:S(2)}, u32[]{:S(2)}) async-start(bf16[16,4,512]{2,1,0:T(4,128)(2,1)} %head.1.after), calls=%async_computation | async-start | bytes 131072 | tf_op jit(solution)/shard_map/all_to_all | solution.py:259
  11.6 8.7 %collective-permute-start = (bf16[16,512]{1,0:T(8,128)(2,1)S(1)}, bf16[16,512]{1,0:T(8,128)(2,1)S(1)}, u32[]{:S(2)}, u32[]{:S(2)}) collective-permute-start(bf16[16,512]{1,0:T(8,128)(2,1)S(1)} %get-tuple-element.30), channel_id=1, source_target_pairs={{0,1},{2,3},{4,5},{6,7},{8,9},{10,11},{12,13},{14,15},{1,0},{3,2},... | collective-permute-start | bytes 49160 | tf_op jit(solution)/shard_map/ppermute | solution.py:25
  11.8 8.5 %collective-permute-start.1 = (bf16[16,512]{1,0:T(8,128)(2,1)S(1)}, bf16[16,512]{1,0:T(8,128)(2,1)S(1)}, u32[]{:S(2)}, u32[]{:S(2)}) collective-permute-start(bf16[16,512]{1,0:T(8,128)(2,1)S(1)} %get-tuple-element.32), channel_id=1, source_target_pairs={{1,2},{3,4},{5,6},{7,8},{9,10},{11,12},{13,14},{15,0},{2,1},{4,3},... | collective-permute-start | bytes 49160 | tf_op jit(solution)/shard_map/ppermute | solution.py:25
  15.8 9.0 %all-to-all-start.1 = ((bf16[16,4,512]{2,1,0:T(4,128)(2,1)}), bf16[16,4,512]{2,1,0:T(4,128)(2,1)S(1)}, u32[]{:S(2)}, u32[]{:S(2)}) async-start(bf16[16,4,512]{2,1,0:T(4,128)(2,1)} %get-tuple-element.29.after), calls=%async_computation.1 | async-start | bytes 131072 | tf_op jit(solution)/shard_map/all_to_all | solution.py:294

commit v10 on v9

--- a/solution.py
+++ b/solution.py
@@ -14,7 +14,11 @@
 BF16, F32 = jnp.bfloat16, jnp.float32
 
 
-def order(group, sub):
+def first_order(group, sub):
+    return [(i + group // sub // 2 * sub) % group for i in range(group)]
+
+
+def second_order(group, sub):
     patch = group // sub
     return [(i + patch // 2) % patch * sub + j for j in range(sub) for i in range(patch)]
 
@@ -98,10 +102,7 @@
     part_ref[...] = dot(cedges_ref[...], w_self_ref[...])
     rows, ids = picks_ref.shape
     at = lax.broadcasted_iota(jnp.int32, (rows, ids), 0)
-    sub, patch = lax.axis_size("sub"), lax.axis_size("patch")
-    block = at // CO_DEV
-    device = (block % patch + patch // 2) % patch * sub + block // patch
-    node = device * CO_DEV + at % CO_DEV
+    node = (at + CO_DEV * first_order(rows // CO_DEV, lax.axis_size("sub"))[0]) % rows
     send = jnp.where(node == csend_ref[...], 1.0, 0.0).astype(BF16)
     recv = jnp.where(node == crecv_ref[...], 1.0, 0.0).astype(BF16)
     picks_ref[...] = onehot_t(rows, crecv_ref[...])
@@ -126,7 +127,7 @@
     new = (edges_ref[...].astype(F32) + centred * scale).astype(BF16)
     new_ref[...] = new
     sums = dot(picks_ref[...], new).astype(BF16)
-    for at, owner in enumerate(order(blocks, lax.axis_size("sub"))):
+    for at, owner in enumerate(second_order(blocks, lax.axis_size("sub"))):
         sums_ref[at] = sums[owner * CO_DEV : (owner + 1) * CO_DEV, :]
 
 
@@ -256,7 +257,7 @@
     (heads,) = call(
         head_kernel, "head", (blocks,), in_hbm(node_latents), hbm=(0,), scratch=[vmem((TOP, width), BF16), dma(())],
     )
-    lat = lax.all_to_all(heads, GROUP_AXES, 0, 0, axis_index_groups=[order(group, sub)])
+    lat = lax.all_to_all(heads, GROUP_AXES, 0, 0, axis_index_groups=[first_order(group, sub)])
     send, recv = ids(fine_senders), ids(fine_receivers)
     nodes, cedges, w_ends, w_out, send, recv, to_even, to_odd, gather, picks, coarse_part = call(
         load_kernel,
@@ -291,7 +292,7 @@
         coarse_kernel, "coarse", (like(coarse_edges), blocks),
         [lat, cedges, coarse_part, gather, picks, w_ends, w_out],
     )
-    got = lax.all_to_all(sums, GROUP_AXES, 0, 0, axis_index_groups=[order(group, sub)])
+    got = lax.all_to_all(sums, GROUP_AXES, 0, 0, axis_index_groups=[second_order(group, sub)])
     new_edges, new_coarse, rest, agg, node_part, wn_agg, wn_out = call(
         fine_kernel,
         "fine",

time: 26.3 us -> 26.3 us (level)
  no operation moved by 1% of the time
where the time goes in v10:
time: 26.3 us; the launch traced here: 25.9 us
  starting transfers between devices  14.7 us (56%)
  Pallas kernels  9.83 us (37%)
  waiting for transfers between devices  0.74 us (3%)
  between operations  0.67 us (3%)
    pallas_call x5, Pallas kernels, call(): pl.pallas_call(kernel, out_shape=outs, in_specs=[ANY if i in hbm else VME...  9.83 us
    all_to_all x1, starting transfers between devices, body(): lax.all_to_all(heads, GROUP_AXES, 0, 0, axis_index_groups=[first_order(gr...  7.84 us
    all_to_all x1, starting transfers between devices, body(): lax.all_to_all(sums, GROUP_AXES, 0, 0, axis_index_groups=[second_order(gr...  4.33 us
    ppermute x2, starting transfers between devices, pair(): return lax.ppermute(value, GROUP_AXES, pairs + [(b, a) for a, b in pairs])  2.54 us
  transfers between devices with their start and end apart: 4, of which 2 were waited for; matrix products, arithmetic and copies ran while one was open for 0% of the time, Pallas kernels for 28%

profile of v10, /device:TPU:0, one launch (start us, length us, event | category | flops | bytes accessed | tf_op | source)
XLA Modules:
  0.0 25.9 jit_solution(4690633479331777936)
XLA Ops:
  0.6 1.4 %head.1.after = bf16[16,4,512]{2,1,0:T(4,128)(2,1)} custom-call(bf16[128,512]{1,0:T(8,128)(2,1)} %nodes_hbm.3), custom_call_target="tpu_custom_call" | custom-call | tf_op jit(solution)/shard_map/head/pallas_call | solution.py:215
  2.0 7.8 %all-to-all-start = ((bf16[16,4,512]{2,1,0:T(4,128)(2,1)}), bf16[16,4,512]{2,1,0:T(4,128)(2,1)S(1)}, u32[]{:S(2)}, u32[]{:S(2)}) async-start(bf16[16,4,512]{2,1,0:T(4,128)(2,1)} %head.1.after), calls=%async_computation | async-start | bytes 131072 | tf_op jit(solution)/shard_map/all_to_all | solution.py:260
  9.8 1.8 %load.1 = (bf16[128,512]{1,0:T(8,128)(2,1)S(1)}, bf16[64,512]{1,0:T(8,128)(2,1)S(1)}, bf16[1024,512]{1,0:T(8,128)(2,1)S(1)}, bf16[512,512]{1,0:T(8,128)(2,1)S(1)...) custom-call(bf16[128,512]{1,0:T(8,128)(2,1)} %nodes_hbm.3, ...), custom_call_target="tpu_custom_call" | custom-call | flops 268435456 | tf_op jit(solution)/shard_map/load/pallas_call | solution.py:215
  11.6 0.2 collective-permute-start
  11.8 2.3 %collective-permute-start.1 = (bf16[16,512]{1,0:T(8,128)(2,1)S(1)}, bf16[16,512]{1,0:T(8,128)(2,1)S(1)}, u32[]{:S(2)}, u32[]{:S(2)}) collective-permute-start(bf16[16,512]{1,0:T(8,128)(2,1)S(1)} %get-tuple-element.32), channel_id=1, source_target_pairs={{1,2},{3,4},{5,6},{7,8},{9,10},{11,12},{13,14},{15,0},{2,1},{4,3},... | collective-permute-start | bytes 49160 | tf_op jit(solution)/shard_map/ppermute | solution.py:29
  14.2 0.3 %all-to-all-done.lat_ref = bf16[16,4,512]{2,1,0:T(4,128)(2,1)S(1)} async-done(((bf16[16,4,512]{2,1,0:T(4,128)(2,1)}), bf16[16,4,512]{2,1,0:T(4,128)(2,1)S(1)}, u32[]{:S(2)}, u32[]{:S(2)}) %all-to-all-start) | async-done | bytes 65568 | tf_op jit(solution)/shard_map/all_to_all | solution.py:260
  14.5 1.5 %coarse.1 = (bf16[64,512]{1,0:T(8,128)(2,1)S(1)}, bf16[16,4,512]{2,1,0:T(4,128)(2,1)}) custom-call(bf16[16,4,512]{2,1,0:T(4,128)(2,1)S(1)} %all-to-all-done.lat_ref, bf16[64,512]{1,0:T(8,128)(2,1)S(1)} %get-tuple-element.23.edges_ref, f32[64,512]{1,0:T(8,128)S(1)} %get-tuple-element.24.part_ref, bf16[128,64]{1,0:T(8,128)(2,1)S(1)} %get-tuple-element.25.gather_ref, ...), custom_call_target="tpu_custom_call" | custom-call | tf_op jit(solution)/shard_map/coarse/pallas_call | solution.py:215
  16.0 4.3 %all-to-all-start.1 = ((bf16[16,4,512]{2,1,0:T(4,128)(2,1)}), bf16[16,4,512]{2,1,0:T(4,128)(2,1)S(1)}, u32[]{:S(2)}, u32[]{:S(2)}) async-start(bf16[16,4,512]{2,1,0:T(4,128)(2,1)} %get-tuple-element.29.after), calls=%async_computation.1 | async-start | bytes 131072 | tf_op jit(solution)/shard_map/all_to_all | solution.py:295
  20.3 0.0 collective-permute-done.even_ref
  20.3 0.0 collective-permute-done.1.odd_ref
  20.3 4.1 %fine.1 = (bf16[512,512]{1,0:T(8,128)(2,1)}, bf16[64,512]{1,0:T(8,128)(2,1)}, bf16[128,512]{1,0:T(8,128)(2,1)S(1)}, f32[16,512]{1,0:T(8,128)S(1)}, f32[16,512]{1...) custom-call(bf16[16,512]{1,0:T(8,128)(2,1)S(1)} %collective-permute-done.even_ref, ...), custom_call_target="tpu_custom_call" | custom-call | flops 17179869184 | tf_op jit(solution)/shard_map/fine/pallas_call | solution.py:215
  24.4 0.4 %all-to-all-done.1.got_ref = bf16[16,4,512]{2,1,0:T(4,128)(2,1)S(1)} async-done(((bf16[16,4,512]{2,1,0:T(4,128)(2,1)}), bf16[16,4,512]{2,1,0:T(4,128)(2,1)S(1)}, u32[]{:S(2)}, u32[]{:S(2)}) %all-to-all-start.1) | async-done | bytes 65568 | tf_op jit(solution)/shard_map/all_to_all | solution.py:295
  24.8 1.1 %top.1 = bf16[128,512]{1,0:T(8,128)(2,1)} custom-call(bf16[16,4,512]{2,1,0:T(4,128)(2,1)S(1)} %all-to-all-done.1.got_ref, f32[16,512]{1,0:T(8,128)S(1)} %get-tuple-element.36.agg_ref, f32[16,512]{1,0:T(8,128)S(1)} %get-tuple-element.37.part_ref, bf16[128,512]{1,0:T(8,128)(2,1)S(1)} %get-tuple-element.31.nodes_ref, ...), custom_call_target="tpu_custom_call" | custom-call | tf_op jit(solution)/shard_map/top/pallas_call | solution.py:215
Async XLA Ops:
  2.0 12.5 %all-to-all-start = ((bf16[16,4,512]{2,1,0:T(4,128)(2,1)}), bf16[16,4,512]{2,1,0:T(4,128)(2,1)S(1)}, u32[]{:S(2)}, u32[]{:S(2)}) async-start(bf16[16,4,512]{2,1,0:T(4,128)(2,1)} %head.1.after), calls=%async_computation | async-start | bytes 131072 | tf_op jit(solution)/shard_map/all_to_all | solution.py:260
  11.6 8.7 %collective-permute-start = (bf16[16,512]{1,0:T(8,128)(2,1)S(1)}, bf16[16,512]{1,0:T(8,128)(2,1)S(1)}, u32[]{:S(2)}, u32[]{:S(2)}) collective-permute-start(bf16[16,512]{1,0:T(8,128)(2,1)S(1)} %get-tuple-element.30), channel_id=1, source_target_pairs={{0,1},{2,3},{4,5},{6,7},{8,9},{10,11},{12,13},{14,15},{1,0},{3,2},... | collective-permute-start | bytes 49160 | tf_op jit(solution)/shard_map/ppermute | solution.py:29
  11.8 8.5 %collective-permute-start.1 = (bf16[16,512]{1,0:T(8,128)(2,1)S(1)}, bf16[16,512]{1,0:T(8,128)(2,1)S(1)}, u32[]{:S(2)}, u32[]{:S(2)}) collective-permute-start(bf16[16,512]{1,0:T(8,128)(2,1)S(1)} %get-tuple-element.32), channel_id=1, source_target_pairs={{1,2},{3,4},{5,6},{7,8},{9,10},{11,12},{13,14},{15,0},{2,1},{4,3},... | collective-permute-start | bytes 49160 | tf_op jit(solution)/shard_map/ppermute | solution.py:29
  16.0 8.8 %all-to-all-start.1 = ((bf16[16,4,512]{2,1,0:T(4,128)(2,1)}), bf16[16,4,512]{2,1,0:T(4,128)(2,1)S(1)}, u32[]{:S(2)}, u32[]{:S(2)}) async-start(bf16[16,4,512]{2,1,0:T(4,128)(2,1)} %get-tuple-element.29.after), calls=%async_computation.1 | async-start | bytes 131072 | tf_op jit(solution)/shard_map/all_to_all | solution.py:295

commit v11 on v9

--- a/solution.py
+++ b/solution.py
@@ -131,7 +131,7 @@
 
 
 def fine_kernel(
-    even_ref, nodes_ref, odd_ref, w_ends_ref, w_out_ref, send_ref, recv_ref, coarse_ref,
+    odd_ref, nodes_ref, even_ref, w_ends_ref, w_out_ref, send_ref, recv_ref, coarse_ref,
     edges_hbm, w_in_hbm, wn_in_hbm, wn_out_hbm, after,
     new_hbm, coarse_hbm, out_ref, agg_ref, npart_ref, wn_agg_ref, wn_out_ref,
     edges_ref, w_self_ref, wn_self_ref, new_ref, sems, out_sems,
@@ -286,7 +286,7 @@
         ],
         flops=edge_count * square,
     )
-    from_even, from_odd = pair(to_even, 0), pair(to_odd, 1)
+    from_odd, from_even = pair(to_odd, 1), pair(to_even, 0)
     new_coarse, sums = call(
         coarse_kernel, "coarse", (like(coarse_edges), blocks),
         [lat, cedges, coarse_part, gather, picks, w_ends, w_out],
@@ -304,7 +304,7 @@
             shape((width, width), BF16),
             like(w_node_out),
         ),
-        [from_even, nodes, from_odd, w_ends, w_out, send, recv, new_coarse]
+        [from_odd, nodes, from_even, w_ends, w_out, send, recv, new_coarse]
         + in_hbm(edge_latents, w_edge_in, w_node_in, w_node_out)
         + [sums],
         hbm=range(8, 13),

time: 26.3 us -> 26.4 us (level)
  waiting for transfers between devices: 0.56 us -> 0.92 us
    ppermute x2, starting transfers between devices: 2.54 us -> 2.19 us  [pair(): return lax.ppermute(value, GROUP_AXES, pairs + [(b, a) for a, b in pairs])]
    all_to_all x1, waiting for transfers between devices: 0.15 us -> 0.5 us  [body(): lax.all_to_all(heads, GROUP_AXES, 0, 0, axis_index_groups=[order(group, s...]
where the time goes in v11:
time: 26.4 us; the launch traced here: 26 us
  starting transfers between devices  14.6 us (55%)
  Pallas kernels  9.84 us (37%)
  waiting for transfers between devices  0.92 us (3%)
  between operations  0.67 us (3%)
    pallas_call x5, Pallas kernels, call(): pl.pallas_call(kernel, out_shape=outs, in_specs=[ANY if i in hbm else VME...  9.84 us
    all_to_all x1, starting transfers between devices, body(): lax.all_to_all(heads, GROUP_AXES, 0, 0, axis_index_groups=[order(group, s...  7.84 us
    all_to_all x1, starting transfers between devices, body(): lax.all_to_all(sums, GROUP_AXES, 0, 0, axis_index_groups=[order(group, su...  4.54 us
    ppermute x2, starting transfers between devices, pair(): return lax.ppermute(value, GROUP_AXES, pairs + [(b, a) for a, b in pairs])  2.19 us
  transfers between devices with their start and end apart: 4, of which 2 were waited for; matrix products, arithmetic and copies ran while one was open for 0% of the time, Pallas kernels for 28%

profile of v11, /device:TPU:0, one launch (start us, length us, event | category | flops | bytes accessed | tf_op | source)
XLA Modules:
  0.0 26.0 jit_solution(8458208455569449245)
XLA Ops:
  0.6 1.4 %head.1.after = bf16[16,4,512]{2,1,0:T(4,128)(2,1)} custom-call(bf16[128,512]{1,0:T(8,128)(2,1)} %nodes_hbm.3), custom_call_target="tpu_custom_call" | custom-call | tf_op jit(solution)/shard_map/head/pallas_call | solution.py:214
  2.0 7.8 %all-to-all-start = ((bf16[16,4,512]{2,1,0:T(4,128)(2,1)}), bf16[16,4,512]{2,1,0:T(4,128)(2,1)S(1)}, u32[]{:S(2)}, u32[]{:S(2)}) async-start(bf16[16,4,512]{2,1,0:T(4,128)(2,1)} %head.1.after), calls=%async_computation | async-start | bytes 131072 | tf_op jit(solution)/shard_map/all_to_all | solution.py:259
  9.8 1.8 %load.1 = (bf16[128,512]{1,0:T(8,128)(2,1)S(1)}, bf16[64,512]{1,0:T(8,128)(2,1)S(1)}, bf16[1024,512]{1,0:T(8,128)(2,1)S(1)}, bf16[512,512]{1,0:T(8,128)(2,1)S(1)...) custom-call(bf16[128,512]{1,0:T(8,128)(2,1)} %nodes_hbm.3, ...), custom_call_target="tpu_custom_call" | custom-call | flops 268435456 | tf_op jit(solution)/shard_map/load/pallas_call | solution.py:214
  11.6 2.2 %collective-permute-start = (bf16[16,512]{1,0:T(8,128)(2,1)S(1)}, bf16[16,512]{1,0:T(8,128)(2,1)S(1)}, u32[]{:S(2)}, u32[]{:S(2)}) collective-permute-start(bf16[16,512]{1,0:T(8,128)(2,1)S(1)} %get-tuple-element.30), channel_id=1, source_target_pairs={{1,2},{3,4},{5,6},{7,8},{9,10},{11,12},{13,14},{15,0},{2,1},{4,3},... | collective-permute-start | bytes 49160 | tf_op jit(solution)/shard_map/ppermute | solution.py:25
  13.8 0.0 collective-permute-start.1
  13.8 0.5 %all-to-all-done.lat_ref = bf16[16,4,512]{2,1,0:T(4,128)(2,1)S(1)} async-done(((bf16[16,4,512]{2,1,0:T(4,128)(2,1)}), bf16[16,4,512]{2,1,0:T(4,128)(2,1)S(1)}, u32[]{:S(2)}, u32[]{:S(2)}) %all-to-all-start) | async-done | bytes 65568 | tf_op jit(solution)/shard_map/all_to_all | solution.py:259
  14.3 1.5 %coarse.1 = (bf16[64,512]{1,0:T(8,128)(2,1)S(1)}, bf16[16,4,512]{2,1,0:T(4,128)(2,1)}) custom-call(bf16[16,4,512]{2,1,0:T(4,128)(2,1)S(1)} %all-to-all-done.lat_ref, bf16[64,512]{1,0:T(8,128)(2,1)S(1)} %get-tuple-element.23.edges_ref, f32[64,512]{1,0:T(8,128)S(1)} %get-tuple-element.24.part_ref, bf16[128,64]{1,0:T(8,128)(2,1)S(1)} %get-tuple-element.25.gather_ref, ...), custom_call_target="tpu_custom_call" | custom-call | tf_op jit(solution)/shard_map/coarse/pallas_call | solution.py:214
  15.8 4.5 %all-to-all-start.1 = ((bf16[16,4,512]{2,1,0:T(4,128)(2,1)}), bf16[16,4,512]{2,1,0:T(4,128)(2,1)S(1)}, u32[]{:S(2)}, u32[]{:S(2)}) async-start(bf16[16,4,512]{2,1,0:T(4,128)(2,1)} %get-tuple-element.29.after), calls=%async_computation.1 | async-start | bytes 131072 | tf_op jit(solution)/shard_map/all_to_all | solution.py:294
  20.4 0.0 collective-permute-done.odd_ref
  20.4 0.0 collective-permute-done.1.even_ref
  20.4 4.1 %fine.1 = (bf16[512,512]{1,0:T(8,128)(2,1)}, bf16[64,512]{1,0:T(8,128)(2,1)}, bf16[128,512]{1,0:T(8,128)(2,1)S(1)}, f32[16,512]{1,0:T(8,128)S(1)}, f32[16,512]{1...) custom-call(bf16[16,512]{1,0:T(8,128)(2,1)S(1)} %collective-permute-done.odd_ref, ...), custom_call_target="tpu_custom_call" | custom-call | flops 17179869184 | tf_op jit(solution)/shard_map/fine/pallas_call | solution.py:214
  24.4 0.4 %all-to-all-done.1.got_ref = bf16[16,4,512]{2,1,0:T(4,128)(2,1)S(1)} async-done(((bf16[16,4,512]{2,1,0:T(4,128)(2,1)}), bf16[16,4,512]{2,1,0:T(4,128)(2,1)S(1)}, u32[]{:S(2)}, u32[]{:S(2)}) %all-to-all-start.1) | async-done | bytes 65568 | tf_op jit(solution)/shard_map/all_to_all | solution.py:294
  24.9 1.1 %top.1 = bf16[128,512]{1,0:T(8,128)(2,1)} custom-call(bf16[16,4,512]{2,1,0:T(4,128)(2,1)S(1)} %all-to-all-done.1.got_ref, f32[16,512]{1,0:T(8,128)S(1)} %get-tuple-element.36.agg_ref, f32[16,512]{1,0:T(8,128)S(1)} %get-tuple-element.37.part_ref, bf16[128,512]{1,0:T(8,128)(2,1)S(1)} %get-tuple-element.31.nodes_ref, ...), custom_call_target="tpu_custom_call" | custom-call | tf_op jit(solution)/shard_map/top/pallas_call | solution.py:214
Async XLA Ops:
  2.0 12.3 %all-to-all-start = ((bf16[16,4,512]{2,1,0:T(4,128)(2,1)}), bf16[16,4,512]{2,1,0:T(4,128)(2,1)S(1)}, u32[]{:S(2)}, u32[]{:S(2)}) async-start(bf16[16,4,512]{2,1,0:T(4,128)(2,1)} %head.1.after), calls=%async_computation | async-start | bytes 131072 | tf_op jit(solution)/shard_map/all_to_all | solution.py:259
  11.6 8.8 %collective-permute-start = (bf16[16,512]{1,0:T(8,128)(2,1)S(1)}, bf16[16,512]{1,0:T(8,128)(2,1)S(1)}, u32[]{:S(2)}, u32[]{:S(2)}) collective-permute-start(bf16[16,512]{1,0:T(8,128)(2,1)S(1)} %get-tuple-element.30), channel_id=1, source_target_pairs={{1,2},{3,4},{5,6},{7,8},{9,10},{11,12},{13,14},{15,0},{2,1},{4,3},... | collective-permute-start | bytes 49160 | tf_op jit(solution)/shard_map/ppermute | solution.py:25
  13.8 6.6 %collective-permute-start.1 = (bf16[16,512]{1,0:T(8,128)(2,1)S(1)}, bf16[16,512]{1,0:T(8,128)(2,1)S(1)}, u32[]{:S(2)}, u32[]{:S(2)}) collective-permute-start(bf16[16,512]{1,0:T(8,128)(2,1)S(1)} %get-tuple-element.32), channel_id=1, source_target_pairs={{0,1},{2,3},{4,5},{6,7},{8,9},{10,11},{12,13},{14,15},{1,0},{3,2},... | collective-permute-start | bytes 49160 | tf_op jit(solution)/shard_map/ppermute | solution.py:25
  15.8 9.0 %all-to-all-start.1 = ((bf16[16,4,512]{2,1,0:T(4,128)(2,1)}), bf16[16,4,512]{2,1,0:T(4,128)(2,1)S(1)}, u32[]{:S(2)}, u32[]{:S(2)}) async-start(bf16[16,4,512]{2,1,0:T(4,128)(2,1)} %get-tuple-element.29.after), calls=%async_computation.1 | async-start | bytes 131072 | tf_op jit(solution)/shard_map/all_to_all | solution.py:294

commit v12 on v9

--- a/solution.py
+++ b/solution.py
@@ -14,9 +14,9 @@
 BF16, F32 = jnp.bfloat16, jnp.float32
 
 
-def order(group, sub):
+def order(group, sub, first=0):
     patch = group // sub
-    return [(i + patch // 2) % patch * sub + j for j in range(sub) for i in range(patch)]
+    return [(i + patch // 2) % patch * sub + (j + first) % sub for j in range(sub) for i in range(patch)]
 
 
 def pair(value, first):
@@ -100,7 +100,7 @@
     at = lax.broadcasted_iota(jnp.int32, (rows, ids), 0)
     sub, patch = lax.axis_size("sub"), lax.axis_size("patch")
     block = at // CO_DEV
-    device = (block % patch + patch // 2) % patch * sub + block // patch
+    device = (block % patch + patch // 2) % patch * sub + (block // patch + sub // 2) % sub
     node = device * CO_DEV + at % CO_DEV
     send = jnp.where(node == csend_ref[...], 1.0, 0.0).astype(BF16)
     recv = jnp.where(node == crecv_ref[...], 1.0, 0.0).astype(BF16)
@@ -256,7 +256,7 @@
     (heads,) = call(
         head_kernel, "head", (blocks,), in_hbm(node_latents), hbm=(0,), scratch=[vmem((TOP, width), BF16), dma(())],
     )
-    lat = lax.all_to_all(heads, GROUP_AXES, 0, 0, axis_index_groups=[order(group, sub)])
+    lat = lax.all_to_all(heads, GROUP_AXES, 0, 0, axis_index_groups=[order(group, sub, sub // 2)])
     send, recv = ids(fine_senders), ids(fine_receivers)
     nodes, cedges, w_ends, w_out, send, recv, to_even, to_odd, gather, picks, coarse_part = call(
         load_kernel,

time: 26.3 us -> 26.5 us (level)
  starting transfers between devices: 14.8 us -> 15.1 us
    ppermute x2, starting transfers between devices: 2.54 us -> 1.58 us  [pair(): return lax.ppermute(value, GROUP_AXES, pairs + [(b, a) for a, b in pairs])]
    all_to_all x1, starting transfers between devices: 4.45 us -> 5.17 us  [body(): lax.all_to_all(sums, GROUP_AXES, 0, 0, axis_index_groups=[order(group, su...]
    all_to_all x1, starting transfers between devices: 7.84 us -> 8.33 us  [body(): lax.all_to_all(heads, GROUP_AXES, 0, 0, axis_index_groups=[order(group, s...]
where the time goes in v12:
time: 26.5 us; the launch traced here: 26.1 us
  starting transfers between devices  15.1 us (57%)
  Pallas kernels  9.83 us (37%)
  between operations  0.67 us (3%)
  waiting for transfers between devices  0.53 us (2%)
    pallas_call x5, Pallas kernels, call(): pl.pallas_call(kernel, out_shape=outs, in_specs=[ANY if i in hbm else VME...  9.83 us
    all_to_all x1, starting transfers between devices, body(): lax.all_to_all(heads, GROUP_AXES, 0, 0, axis_index_groups=[order(group, s...  8.33 us
    all_to_all x1, starting transfers between devices, body(): lax.all_to_all(sums, GROUP_AXES, 0, 0, axis_index_groups=[order(group, su...  5.17 us
    ppermute x2, starting transfers between devices, pair(): return lax.ppermute(value, GROUP_AXES, pairs + [(b, a) for a, b in pairs])  1.58 us
  transfers between devices with their start and end apart: 4, of which 2 were waited for; matrix products, arithmetic and copies ran while one was open for 0% of the time, Pallas kernels for 28%

profile of v12, /device:TPU:0, one launch (start us, length us, event | category | flops | bytes accessed | tf_op | source)
XLA Modules:
  0.0 26.1 jit_solution(13478459216612367210)
XLA Ops:
  0.6 1.4 %head.1.after = bf16[16,4,512]{2,1,0:T(4,128)(2,1)} custom-call(bf16[128,512]{1,0:T(8,128)(2,1)} %nodes_hbm.3), custom_call_target="tpu_custom_call" | custom-call | tf_op jit(solution)/shard_map/head/pallas_call | solution.py:214
  2.0 8.3 %all-to-all-start = ((bf16[16,4,512]{2,1,0:T(4,128)(2,1)}), bf16[16,4,512]{2,1,0:T(4,128)(2,1)S(1)}, u32[]{:S(2)}, u32[]{:S(2)}) async-start(bf16[16,4,512]{2,1,0:T(4,128)(2,1)} %head.1.after), calls=%async_computation | async-start | bytes 131072 | tf_op jit(solution)/shard_map/all_to_all | solution.py:259
  10.3 1.8 %load.1 = (bf16[128,512]{1,0:T(8,128)(2,1)S(1)}, bf16[64,512]{1,0:T(8,128)(2,1)S(1)}, bf16[1024,512]{1,0:T(8,128)(2,1)S(1)}, bf16[512,512]{1,0:T(8,128)(2,1)S(1)...) custom-call(bf16[128,512]{1,0:T(8,128)(2,1)} %nodes_hbm.3, ...), custom_call_target="tpu_custom_call" | custom-call | flops 268435456 | tf_op jit(solution)/shard_map/load/pallas_call | solution.py:214
  12.1 0.2 collective-permute-start
  12.3 1.4 %collective-permute-start.1 = (bf16[16,512]{1,0:T(8,128)(2,1)S(1)}, bf16[16,512]{1,0:T(8,128)(2,1)S(1)}, u32[]{:S(2)}, u32[]{:S(2)}) collective-permute-start(bf16[16,512]{1,0:T(8,128)(2,1)S(1)} %get-tuple-element.32), channel_id=1, source_target_pairs={{1,2},{3,4},{5,6},{7,8},{9,10},{11,12},{13,14},{15,0},{2,1},{4,3},... | collective-permute-start | bytes 49160 | tf_op jit(solution)/shard_map/ppermute | solution.py:25
  13.7 0.1 all-to-all-done.lat_ref
  13.8 1.5 %coarse.1 = (bf16[64,512]{1,0:T(8,128)(2,1)S(1)}, bf16[16,4,512]{2,1,0:T(4,128)(2,1)}) custom-call(bf16[16,4,512]{2,1,0:T(4,128)(2,1)S(1)} %all-to-all-done.lat_ref, bf16[64,512]{1,0:T(8,128)(2,1)S(1)} %get-tuple-element.23.edges_ref, f32[64,512]{1,0:T(8,128)S(1)} %get-tuple-element.24.part_ref, bf16[128,64]{1,0:T(8,128)(2,1)S(1)} %get-tuple-element.25.gather_ref, ...), custom_call_target="tpu_custom_call" | custom-call | tf_op jit(solution)/shard_map/coarse/pallas_call | solution.py:214
  15.3 5.2 %all-to-all-start.1 = ((bf16[16,4,512]{2,1,0:T(4,128)(2,1)}), bf16[16,4,512]{2,1,0:T(4,128)(2,1)S(1)}, u32[]{:S(2)}, u32[]{:S(2)}) async-start(bf16[16,4,512]{2,1,0:T(4,128)(2,1)} %get-tuple-element.29.after), calls=%async_computation.1 | async-start | bytes 131072 | tf_op jit(solution)/shard_map/all_to_all | solution.py:294
  20.5 0.0 collective-permute-done.even_ref
  20.5 0.0 collective-permute-done.1.odd_ref
  20.5 4.1 %fine.1 = (bf16[512,512]{1,0:T(8,128)(2,1)}, bf16[64,512]{1,0:T(8,128)(2,1)}, bf16[128,512]{1,0:T(8,128)(2,1)S(1)}, f32[16,512]{1,0:T(8,128)S(1)}, f32[16,512]{1...) custom-call(bf16[16,512]{1,0:T(8,128)(2,1)S(1)} %collective-permute-done.even_ref, ...), custom_call_target="tpu_custom_call" | custom-call | flops 17179869184 | tf_op jit(solution)/shard_map/fine/pallas_call | solution.py:214
  24.6 0.4 %all-to-all-done.1.got_ref = bf16[16,4,512]{2,1,0:T(4,128)(2,1)S(1)} async-done(((bf16[16,4,512]{2,1,0:T(4,128)(2,1)}), bf16[16,4,512]{2,1,0:T(4,128)(2,1)S(1)}, u32[]{:S(2)}, u32[]{:S(2)}) %all-to-all-start.1) | async-done | bytes 65568 | tf_op jit(solution)/shard_map/all_to_all | solution.py:294
  25.0 1.1 %top.1 = bf16[128,512]{1,0:T(8,128)(2,1)} custom-call(bf16[16,4,512]{2,1,0:T(4,128)(2,1)S(1)} %all-to-all-done.1.got_ref, f32[16,512]{1,0:T(8,128)S(1)} %get-tuple-element.36.agg_ref, f32[16,512]{1,0:T(8,128)S(1)} %get-tuple-element.37.part_ref, bf16[128,512]{1,0:T(8,128)(2,1)S(1)} %get-tuple-element.31.nodes_ref, ...), custom_call_target="tpu_custom_call" | custom-call | tf_op jit(solution)/shard_map/top/pallas_call | solution.py:214
Async XLA Ops:
  2.0 11.8 %all-to-all-start = ((bf16[16,4,512]{2,1,0:T(4,128)(2,1)}), bf16[16,4,512]{2,1,0:T(4,128)(2,1)S(1)}, u32[]{:S(2)}, u32[]{:S(2)}) async-start(bf16[16,4,512]{2,1,0:T(4,128)(2,1)} %head.1.after), calls=%async_computation | async-start | bytes 131072 | tf_op jit(solution)/shard_map/all_to_all | solution.py:259
  12.1 8.4 %collective-permute-start = (bf16[16,512]{1,0:T(8,128)(2,1)S(1)}, bf16[16,512]{1,0:T(8,128)(2,1)S(1)}, u32[]{:S(2)}, u32[]{:S(2)}) collective-permute-start(bf16[16,512]{1,0:T(8,128)(2,1)S(1)} %get-tuple-element.30), channel_id=1, source_target_pairs={{0,1},{2,3},{4,5},{6,7},{8,9},{10,11},{12,13},{14,15},{1,0},{3,2},... | collective-permute-start | bytes 49160 | tf_op jit(solution)/shard_map/ppermute | solution.py:25
  12.3 8.2 %collective-permute-start.1 = (bf16[16,512]{1,0:T(8,128)(2,1)S(1)}, bf16[16,512]{1,0:T(8,128)(2,1)S(1)}, u32[]{:S(2)}, u32[]{:S(2)}) collective-permute-start(bf16[16,512]{1,0:T(8,128)(2,1)S(1)} %get-tuple-element.32), channel_id=1, source_target_pairs={{1,2},{3,4},{5,6},{7,8},{9,10},{11,12},{13,14},{15,0},{2,1},{4,3},... | collective-permute-start | bytes 49160 | tf_op jit(solution)/shard_map/ppermute | solution.py:25
  15.3 9.6 %all-to-all-start.1 = ((bf16[16,4,512]{2,1,0:T(4,128)(2,1)}), bf16[16,4,512]{2,1,0:T(4,128)(2,1)S(1)}, u32[]{:S(2)}, u32[]{:S(2)}) async-start(bf16[16,4,512]{2,1,0:T(4,128)(2,1)} %get-tuple-element.29.after), calls=%async_computation.1 | async-start | bytes 131072 | tf_op jit(solution)/shard_map/all_to_all | solution.py:294
